TPU v7x, 32 devices: a whole 2x2x4 slice. The times are simulated.
32 devices in a mesh: exam: 2 (over x), slab: 16 (over z, y, core).
Axes of the slice: x: 2, y: 2, z: 4, core: 2. Of those that a mesh axis runs over, the one named last changes fastest.
Arguments:
- measured: bfloat16 [4, 16, 128, 16, 320], P('exam', None, None, 'slab'), parts along dimension 0, may hold values from -6 to 6
- coil_maps: bfloat16 [4, 16, 128, 16, 320], P('exam', None, 'slab'), parts along dimension 0, may hold values from -2.5 to 2.5
- start_image: float32 [4, 128, 16, 320], P('exam', 'slab'), parts along dimension 0, may hold values from -6 to 6
- line_mask: int32 [256, 320], P('exam'), parts along dimension 0, may hold values 0 or 1
- conv_plane: bfloat16 [32, 2, 3, 3], replicated, may hold values from -1.5 to 1.5
- conv_depth: bfloat16 [32, 3, 32], replicated, may hold values from -0.625 to 0.625
- conv_output: bfloat16 [2, 32], replicated, may hold values from -1 to 1
Outputs:
- final_image: float32 [4, 128, 16, 320], P('exam', 'slab'), parts along dimension 0
There are 2 independent parts, one for each index of `exam`. A program takes and returns all parts, laid end to end along the dimension named above; an argument that names none is the same for every part. Nothing has to cross between parts.
All inputs are finite; a program needn't handle non-finite values.
Results may differ from a plain program's by a relative error of at most 0.015.
Values may be sent and summed in bfloat16 or wider, within the bound.
A program may use at most 128 MiB of HBM per device.

v0:
```python
import math

import jax
import jax.numpy as jnp
from jax import lax
from jax.sharding import PartitionSpec as P

PASSES = 2


def padded_2(array, sides, width):
    for axis, dim in sides:
        size, length = (lax.axis_size(axis), array.shape[dim])
        up = [(i, (i + 1) % size) for i in range(size - 1)]
        down = [(j, i) for i, j in up]
        last = lax.slice_in_dim(array, length - width, length, axis=dim)
        initial = lax.slice_in_dim(array, 0, width, axis=dim)
        before = lax.ppermute(last, axis, up)
        after = lax.ppermute(initial, axis, down)
        array = jnp.concatenate([before, array, after], axis=dim)
    return array


def dft_table(length):
    position = jnp.arange(length, dtype=jnp.int32)
    product_mod = position[:, None] * position[None, :] % length
    angles = product_mod.astype(jnp.float32) * (2.0 * math.pi / length)
    norm_scale = 1.0 / math.sqrt(length)
    cosine = jnp.cos(angles) * norm_scale
    sine = jnp.sin(angles) * norm_scale
    upper_half = jnp.stack([cosine, sine], axis=1)
    lower_half = jnp.stack([-sine, cosine], axis=1)
    return jnp.stack([upper_half, lower_half], axis=0).astype(jnp.bfloat16)


def complex_times(maps, values):
    maps_real = maps[0].astype(jnp.float32)
    maps_imag = maps[1].astype(jnp.float32)
    value_real = values[0].astype(jnp.float32)
    value_imag = values[1].astype(jnp.float32)
    return jnp.stack(
        [
            maps_real * value_real - maps_imag * value_imag,
            maps_real * value_imag + maps_imag * value_real,
        ]
    ).astype(jnp.bfloat16)


def conj_summed(maps, values):
    maps_real = maps[0].astype(jnp.float32)
    maps_imag = maps[1].astype(jnp.float32)
    real_part = jnp.sum(maps_real * values[0] + maps_imag * values[1], axis=0)
    imag_part = jnp.sum(maps_real * values[1] - maps_imag * values[0], axis=0)
    return jnp.stack([real_part, imag_part])


def forward_y(table_y, coil_image):
    return jnp.einsum(
        "pkqn,qcabn->pcabk", table_y, coil_image, preferred_element_type=jnp.float32
    ).astype(jnp.bfloat16)


def inverse_y(table_y, back_z):
    return jnp.einsum("qkpn,qcabk->pcabn", table_y, back_z, preferred_element_type=jnp.float32)


def residual_back(table_z, hybrid, measured, sample_gate):
    predicted = jnp.einsum("pkqn,qcnxy->pckxy", table_z, hybrid, preferred_element_type=jnp.float32)
    residual = (sample_gate * (predicted - measured.astype(jnp.float32))).astype(jnp.bfloat16)
    return jnp.einsum(
        "qkpn,qckxy->pcnxy", table_z, residual, preferred_element_type=jnp.float32
    ).astype(jnp.bfloat16)


def plane_conv(values, conv_plane):
    first = lax.conv_general_dilated(
        values,
        conv_plane,
        (1, 1),
        "SAME",
        dimension_numbers=("CNHW", "OIHW", "CNHW"),
        preferred_element_type=jnp.float32,
    )
    return jax.nn.relu(first).astype(jnp.bfloat16)


def denoise(noisy_low, conv_plane, conv_depth, conv_output):
    act_one = plane_conv(noisy_low, conv_plane)
    padded = padded_2(act_one, (("slab", 1),), 1)
    planes = noisy_low.shape[1]
    mixed = jnp.einsum(
        "oi,izxy->ozxy",
        conv_depth[:, 0, :],
        padded[:, 0:planes],
        preferred_element_type=jnp.float32,
    )
    for offset in range(1, 3):
        mixed = mixed + jnp.einsum(
            "oi,izxy->ozxy",
            conv_depth[:, offset, :],
            padded[:, offset : offset + planes],
            preferred_element_type=jnp.float32,
        )
    act_two = jax.nn.relu(mixed).astype(jnp.bfloat16)
    return jnp.einsum("pi,izxy->pzxy", conv_output, act_two, preferred_element_type=jnp.float32)


def body(measured, coil_maps, start_image, line_mask, conv_plane, conv_depth, conv_output):
    table_y = dft_table(measured.shape[4])
    table_z = dft_table(measured.shape[2])
    sample_gate = line_mask.astype(jnp.float32)[:, None, :]
    estimate = start_image
    for index_pass in range(PASSES):
        image_low = estimate.astype(jnp.bfloat16)
        coil_image = complex_times(coil_maps, image_low[:, None])
        hybrid = forward_y(table_y, coil_image)
        hybrid_read = lax.all_to_all(hybrid, "slab", split_axis=3, concat_axis=2, tiled=True)
        back_z = residual_back(table_z, hybrid_read, measured, sample_gate)
        back_local = lax.all_to_all(back_z, "slab", split_axis=2, concat_axis=3, tiled=True)
        back_y = inverse_y(table_y, back_local)
        gradient = conj_summed(coil_maps, back_y)
        noisy_image = estimate - gradient
        estimate = noisy_image + denoise(
            noisy_image.astype(jnp.bfloat16), conv_plane, conv_depth, conv_output
        )
    return estimate


def solution(mesh):
    in_specs = (
        P("exam", None, None, "slab", None),
        P("exam", None, "slab", None, None),
        P("exam", "slab", None, None),
        P("exam", None),
        P(),
        P(),
        P(),
    )
    out_specs = P("exam", "slab", None, None)
    return jax.shard_map(body, mesh=mesh, in_specs=in_specs, out_specs=out_specs, check_vma=False)
```

profile of v0, /device:TPU:0, one launch (start us, length us, event | category | flops | bytes accessed | tf_op | source)
XLA Modules:
  0.0 565.2 jit_solution(14419823211593610214)
XLA Ops:
  0.0 2.0 fusion.105
  2.0 2.2 negate_convert_fusion
  5.2 3.0 fusion.21
  9.4 2.9 fusion.18
  12.3 4.5 copy.116
  16.7 7.5 %all-to-all-start = ((bf16[2,16,8,16,320]{4,0,2,1,3:T(2,128)(2,1)}), bf16[2,16,8,16,320]{4,0,2,1,3:T(2,128)(2,1)S(1)}, u32[]{:S(2)}, u32[]{:S(2)}) async-start(bf16[2,16,8,16,320]{4,0,2,1,3:T(2,128)(2,1)} %copy.116), calls=%async_computation | async-start | bytes 6291456 | tf_op jit(solution)/shard_map/all_to_all | solution.py:117
  24.9 58.7 %all-to-all-done = bf16[2,16,8,16,320]{4,0,2,1,3:T(2,128)(2,1)S(1)} async-done(((bf16[2,16,8,16,320]{4,0,2,1,3:T(2,128)(2,1)}), bf16[2,16,8,16,320]{4,0,2,1,3:T(2,128)(2,1)S(1)}, u32[]{:S(2)}, u32[]{:S(2)}) %all-to-all-start) | async-done | bytes 2621472 | tf_op jit(solution)/shard_map/all_to_all | solution.py:117
  83.6 4.9 fusion.64
  88.6 8.2 %copy.121 = bf16[2,16,128,1,320]{4,0,1,3,2:T(2,128)(2,1)S(1)} copy(bf16[2,16,128,1,320]{2,4,0,1,3:T(8,128)(2,1)} %fusion.64) | data formatting | bytes 5242880 | tf_op jit(solution)/shard_map/convert_element_type | solution.py:72
  96.8 85.4 %all_to_all.66 = bf16[2,16,128,1,320]{4,0,1,3,2:T(2,128)(2,1)S(1)} all-to-all(bf16[2,16,128,1,320]{4,0,1,3,2:T(2,128)(2,1)S(1)} %copy.121), channel_id=1, replica_groups=mesh['exam'=2,'slab'=16] {'slab'}, dimensions={2} | all-to-all | bytes 5242880 | tf_op jit(solution)/shard_map/all_to_all | solution.py:119
  182.2 5.6 fusion.58
  187.8 1.2 fusion.25
  189.8 5.1 copy.125
  194.9 13.4 %maximum_convert_fusion.1 = bf16[32,8,16,320]{0,1,3,2:T(8,128)(2,1)S(1)} fusion(bf16[2,8,16,320]{1,0,3,2:T(2,128)(2,1)} %copy.125, bf16[32,2,3,3]{0,1,3,2:T(2,128)(2,1)S(1)} %copy-done), kind=kOutput, calls=%fused_computation.1 | convolution fusion | flops 47747072 | bytes 2786432 | tf_op jit(solution)/shard_map/conv_general_dilated | solution.py:76
  208.3 7.1 %fusion.151 = (bf16[32,1,16,320]{0,1,3,2:T(2,128)(2,1)}, bf16[32,1,16,320]{0,1,3,2:T(2,128)(2,1)}) fusion(bf16[32,8,16,320]{0,1,3,2:T(8,128)(2,1)S(1)} %maximum_convert_fusion.1), kind=kLoop, calls=%fused_computation.170 | loop fusion | bytes 1310720 | tf_op jit(solution)/shard_map/slice | solution.py:16
  215.4 5.0 copy.126
  220.4 3.4 collective-permute-start
  223.9 5.0 copy.130
  228.8 1.7 collective-permute-start.1
  230.5 10.7 %fusion.8 = f32[8,16,320,32]{2,3,1,0:T(8,128)} fusion(bf16[32,8,16,320]{0,1,3,2:T(8,128)(2,1)} %copy-done.1, bf16[32,3,32]{2,0,1:T(8,128)(2,1)} %param.12), kind=kOutput, calls=%fused_computation.14 | convolution fusion | flops 83886080 | bytes 15736832 | tf_op jit(solution)/shard_map/oi,izxy->ozxy/dot_general | solution.py:98
  241.3 5.5 copy.127
  246.7 5.5 copy.131
  252.2 18.7 %pad_maximum_fusion.3 = (bf16[32,8,16,320]{0,1,3,2:T(8,128)(2,1)}, bf16[32,8,16,320]{0,1,3,2:T(8,128)(2,1)S(1)}) fusion(bf16[32,8,16,320]{0,1,3,2:T(8,128)(2,1)} %copy-done.1, bf16[32,1,16,320]{0,1,3,2:T(2,128)(2,1)} %copy.127, bf16[32,1,16,320]{0,1,3,2:T(2,128)(2,1)} %copy.131), kind=kLoop, calls=%fused_computation.5 | loop fusion | flops 10485760 | bytes 8519680 | tf_op jit(solution)/shard_map/concatenate | solution.py:20
  271.0 7.4 %fusion.6 = f32[8,16,320,32]{2,3,1,0:T(8,128)} fusion(bf16[32,8,16,320]{0,1,3,2:T(8,128)(2,1)S(1)} %get-tuple-element.16, bf16[32,3,32]{2,0,1:T(8,128)(2,1)} %param.12), kind=kOutput, calls=%fused_computation.12 | convolution fusion | flops 83886080 | bytes 7872512 | tf_op jit(solution)/shard_map/oi,izxy->ozxy/dot_general | solution.py:98
  278.3 12.9 %fusion.56 = f32[8,16,320,2]{2,3,1,0:T(2,128)} fusion(f32[8,16,320,32]{2,3,1,0:T(8,128)} %fusion.6, f32[8,16,320,32]{2,3,1,0:T(8,128)} %fusion.8, bf16[32,8,16,320]{0,1,3,2:T(8,128)(2,1)} %get-tuple-element.15, bf16[32,3,32]{2,0,1:T(8,128)(2,1)} %param.12, bf16[2,32]{1,0:T(2,128)(2,1)S(1)} %copy-done.23), kind=kOutput, calls=%fused_computation.87 | convolution fusion | flops 94371840 | bytes 23404672 | tf_op jit(solution)/shard_map/pi,izxy->pzxy/dot_general | solution.py:105
  291.2 1.0 fusion.106
  292.3 1.2 fusion.29
  293.5 3.3 fusion.19
  296.8 3.0 copy.134
  299.9 75.9 %all_to_all.67 = bf16[2,16,8,16,320]{4,0,2,1,3:T(2,128)(2,1)} all-to-all(bf16[2,16,8,16,320]{4,0,2,1,3:T(2,128)(2,1)S(1)} %copy.134), channel_id=1, replica_groups=mesh['exam'=2,'slab'=16] {'slab'}, dimensions={3} | all-to-all | bytes 5242880 | tf_op jit(solution)/shard_map/all_to_all | solution.py:117
  375.8 5.9 %fusion.65 = bf16[2,16,128,1,320]{2,4,0,1,3:T(8,128)(2,1)} fusion(f32[128,320]{0,1:T(8,128)} %copy-done.20, bf16[2,16,16,8,1,320]{5,0,3,1,2,4:T(2,128)(2,1)} %bitcast.288, bf16[2,16,128,1,320]{2,4,3,1,0:T(8,128)(2,1)} %param.7, bf16[2,128,2,128]{3,1,2,0:T(8,128)(2,1)} %copy-done.21), kind=kOutput, calls=%fused_computation.91 | convolution fusion | flops 1348730880 | bytes 8159232 | tf_op jit(solution)/shard_map/qkpn,qckxy->pcnxy/dot_general | solution.py:70
  381.7 8.7 %copy.138 = bf16[2,16,128,1,320]{4,0,1,3,2:T(2,128)(2,1)} copy(bf16[2,16,128,1,320]{2,4,0,1,3:T(8,128)(2,1)} %fusion.65) | data formatting | bytes 5242880 | tf_op jit(solution)/shard_map/convert_element_type | solution.py:72
  390.4 75.1 %all_to_all.68 = bf16[2,16,128,1,320]{4,0,1,3,2:T(2,128)(2,1)S(1)} all-to-all(bf16[2,16,128,1,320]{4,0,1,3,2:T(2,128)(2,1)} %copy.138), channel_id=1, replica_groups=mesh['exam'=2,'slab'=16] {'slab'}, dimensions={2} | all-to-all | bytes 5242880 | tf_op jit(solution)/shard_map/all_to_all | solution.py:119
  465.5 5.6 fusion.61
  471.1 1.2 fusion.33
  473.2 2.1 copy.142
  475.3 12.6 %maximum_convert_fusion = bf16[32,8,16,320]{0,1,3,2:T(8,128)(2,1)S(1)} fusion(bf16[2,8,16,320]{1,0,3,2:T(2,128)(2,1)S(1)} %copy.142, bf16[32,2,3,3]{0,1,3,2:T(2,128)(2,1)S(1)} %copy-done), kind=kOutput, calls=%fused_computation | convolution fusion | flops 47747072 | bytes 2786432 | tf_op jit(solution)/shard_map/conv_general_dilated | solution.py:76
  487.9 6.7 %fusion.150 = (bf16[32,1,16,320]{0,1,3,2:T(2,128)(2,1)}, bf16[32,1,16,320]{0,1,3,2:T(2,128)(2,1)S(1)}) fusion(bf16[32,8,16,320]{0,1,3,2:T(8,128)(2,1)S(1)} %maximum_convert_fusion), kind=kLoop, calls=%fused_computation.169 | loop fusion | bytes 1310720 | tf_op jit(solution)/shard_map/slice | solution.py:16
  494.6 4.0 copy.143
  498.6 3.4 collective-permute-start.2
  502.1 2.9 copy.147
  504.9 1.3 collective-permute-start.3
  506.2 10.7 %fusion.2 = f32[8,16,320,32]{2,3,1,0:T(8,128)} fusion(bf16[32,8,16,320]{0,1,3,2:T(8,128)(2,1)} %copy-done.2, bf16[32,3,32]{2,0,1:T(8,128)(2,1)S(1)} %copy-done.22), kind=kOutput, calls=%fused_computation.8 | convolution fusion | flops 83886080 | bytes 7872512 | tf_op jit(solution)/shard_map/oi,izxy->ozxy/dot_general | solution.py:98
  516.9 4.7 copy.144
  521.7 5.5 copy.148
  527.1 18.1 %pad_maximum_fusion.1 = (bf16[32,8,16,320]{0,1,3,2:T(8,128)(2,1)}, bf16[32,8,16,320]{0,1,3,2:T(8,128)(2,1)S(1)}) fusion(bf16[32,8,16,320]{0,1,3,2:T(8,128)(2,1)} %copy-done.2, bf16[32,1,16,320]{0,1,3,2:T(2,128)(2,1)S(1)} %copy.144, bf16[32,1,16,320]{0,1,3,2:T(2,128)(2,1)} %copy.148), kind=kLoop, calls=%fused_computation.3 | loop fusion | flops 10485760 | bytes 8519680 | tf_op jit(solution)/shard_map/concatenate | solution.py:20
  545.3 6.7 %fusion = f32[8,16,320,32]{2,3,1,0:T(8,128)} fusion(bf16[32,8,16,320]{0,1,3,2:T(8,128)(2,1)S(1)} %get-tuple-element.12, bf16[32,3,32]{2,0,1:T(8,128)(2,1)S(1)} %copy-done.22), kind=kOutput, calls=%fused_computation.6 | convolution fusion | flops 83886080 | bytes 15736832 | tf_op jit(solution)/shard_map/oi,izxy->ozxy/dot_general | solution.py:98
  551.9 12.2 %fusion.54 = f32[8,16,320,2]{2,3,1,0:T(2,128)S(1)} fusion(f32[8,16,320,32]{2,3,1,0:T(8,128)} %fusion, f32[8,16,320,32]{2,3,1,0:T(8,128)} %fusion.2, bf16[32,8,16,320]{0,1,3,2:T(8,128)(2,1)} %get-tuple-element.11, bf16[32,3,32]{2,0,1:T(8,128)(2,1)S(1)} %copy-done.22, bf16[2,32]{1,0:T(2,128)(2,1)S(1)} %copy-done.23), kind=kOutput, calls=%fused_computation.86 | convolution fusion | flops 94371840 | bytes 13443584 | tf_op jit(solution)/shard_map/pi,izxy->pzxy/dot_general | solution.py:105
  (64 shorter events, 5.4 us)
Async XLA Ops:
  0.0 194.9 %copy-start = (bf16[32,2,3,3]{0,1,3,2:T(2,128)(2,1)S(1)}, bf16[32,2,3,3]{0,1,3,2:T(2,128)(2,1)}, u32[]{:S(2)}) copy-start(bf16[32,2,3,3]{0,1,3,2:T(2,128)(2,1)} %param.11) | copy-start | bytes 3460
  8.4 0.8 copy-start.11
  8.4 1.0 copy-start.15
  16.7 7.5 %copy-start.19 = (s32[128,320]{0,1:T(8,128)S(1)}, s32[128,320]{0,1:T(8,128)}, u32[]{:S(2)}) copy-start(s32[128,320]{0,1:T(8,128)} %param.10) | copy-start | bytes 491524
  16.7 66.9 %all-to-all-start = ((bf16[2,16,8,16,320]{4,0,2,1,3:T(2,128)(2,1)}), bf16[2,16,8,16,320]{4,0,2,1,3:T(2,128)(2,1)S(1)}, u32[]{:S(2)}, u32[]{:S(2)}) async-start(bf16[2,16,8,16,320]{4,0,2,1,3:T(2,128)(2,1)} %copy.116), calls=%async_computation | async-start | bytes 6291456 | tf_op jit(solution)/shard_map/all_to_all | solution.py:117
  24.3 64.3 %copy-start.20 = (f32[128,320]{0,1:T(8,128)}, f32[128,320]{0,1:T(8,128)S(1)}, u32[]{:S(2)}) copy-start(f32[128,320]{0,1:T(8,128)S(1)} %convert_element_type.160) | copy-start | bytes 491524
  24.9 63.7 %copy-start.21 = (bf16[2,128,2,128]{3,1,2,0:T(8,128)(2,1)}, bf16[2,128,2,128]{3,1,2,0:T(8,128)(2,1)S(1)}, u32[]{:S(2)}) copy-start(bf16[2,128,2,128]{3,1,2,0:T(8,128)(2,1)S(1)} %pad_maximum_fusion.4) | copy-start | bytes 393220
  96.8 85.4 %copy-start.12 = (bf16[1,320,2,320]{3,1,2,0:T(8,128)(2,1)S(1)}, bf16[1,320,2,320]{3,1,2,0:T(8,128)(2,1)}, u32[]{:S(2)}) copy-start(bf16[1,320,2,320]{3,1,2,0:T(8,128)(2,1)} %copy-done.11) | copy-start | bytes 1228804
  96.8 85.4 %copy-start.16 = (bf16[1,320,2,320]{3,1,2,0:T(8,128)(2,1)S(1)}, bf16[1,320,2,320]{3,1,2,0:T(8,128)(2,1)}, u32[]{:S(2)}) copy-start(bf16[1,320,2,320]{3,1,2,0:T(8,128)(2,1)} %copy-done.15) | copy-start | bytes 1228804
  182.2 5.6 copy-start.3
  187.8 1.2 copy-start.10
  208.3 7.2 %copy-start.1 = (bf16[32,8,16,320]{0,1,3,2:T(8,128)(2,1)}, bf16[32,8,16,320]{0,1,3,2:T(8,128)(2,1)S(1)}, u32[]{:S(2)}) copy-start(bf16[32,8,16,320]{0,1,3,2:T(8,128)(2,1)S(1)} %maximum_convert_fusion.1) | copy-start | bytes 7864324
  220.4 20.8 %collective-permute-start = (bf16[32,1,16,320]{3,2,1,0:T(8,128)(2,1)}, bf16[32,1,16,320]{3,2,1,0:T(8,128)(2,1)}, u32[]{:S(2)}, u32[]{:S(2)}) collective-permute-start(bf16[32,1,16,320]{3,2,1,0:T(8,128)(2,1)} %copy.126), channel_id=1, source_target_pairs={{0,1},{1,2},{2,3},{3,4},{4,5},{5,6},{6,7},{7,8},{8,9},{9,10},{10,1... | collective-permute-start | bytes 983048 | tf_op jit(solution)/shard_map/ppermute | solution.py:18
  228.8 17.9 %collective-permute-start.1 = (bf16[32,1,16,320]{3,2,1,0:T(8,128)(2,1)}, bf16[32,1,16,320]{3,2,1,0:T(8,128)(2,1)}, u32[]{:S(2)}, u32[]{:S(2)}) collective-permute-start(bf16[32,1,16,320]{3,2,1,0:T(8,128)(2,1)} %copy.130), channel_id=1, source_target_pairs={{1,0},{2,1},{3,2},{4,3},{5,4},{6,5},{7,6},{8,7},{9,8},{10,9},{11,1... | collective-permute-start | bytes 983048 | tf_op jit(solution)/shard_map/ppermute | solution.py:19
  270.9 7.4 %copy-start.23 = (bf16[2,32]{1,0:T(2,128)(2,1)S(1)}, bf16[2,32]{1,0:T(2,128)(2,1)}, u32[]{:S(2)}) copy-start(bf16[2,32]{1,0:T(2,128)(2,1)} %param.13) | copy-start | bytes 388
  292.3 1.2 copy-start.13
  292.3 1.2 copy-start.17
  390.4 75.1 %copy-start.14 = (bf16[1,320,2,320]{3,1,2,0:T(8,128)(2,1)S(1)}, bf16[1,320,2,320]{3,1,2,0:T(8,128)(2,1)}, u32[]{:S(2)}) copy-start(bf16[1,320,2,320]{3,1,2,0:T(8,128)(2,1)} %copy-done.11) | copy-start | bytes 1228804
  390.4 75.1 %copy-start.18 = (bf16[1,320,2,320]{3,1,2,0:T(8,128)(2,1)S(1)}, bf16[1,320,2,320]{3,1,2,0:T(8,128)(2,1)}, u32[]{:S(2)}) copy-start(bf16[1,320,2,320]{3,1,2,0:T(8,128)(2,1)} %copy-done.15) | copy-start | bytes 1228804
  471.1 2.0 copy-start.4
  472.4 0.7 copy-start.6
  472.4 0.8 copy-start.8
  487.9 6.7 %copy-start.2 = (bf16[32,8,16,320]{0,1,3,2:T(8,128)(2,1)}, bf16[32,8,16,320]{0,1,3,2:T(8,128)(2,1)S(1)}, u32[]{:S(2)}) copy-start(bf16[32,8,16,320]{0,1,3,2:T(8,128)(2,1)S(1)} %maximum_convert_fusion) | copy-start | bytes 7864324
  494.6 11.6 %copy-start.22 = (bf16[32,3,32]{2,0,1:T(8,128)(2,1)S(1)}, bf16[32,3,32]{2,0,1:T(8,128)(2,1)}, u32[]{:S(2)}) copy-start(bf16[32,3,32]{2,0,1:T(8,128)(2,1)} %param.12) | copy-start | bytes 18436
  498.6 18.3 %collective-permute-start.2 = (bf16[32,1,16,320]{3,2,1,0:T(8,128)(2,1)S(1)}, bf16[32,1,16,320]{3,2,1,0:T(8,128)(2,1)}, u32[]{:S(2)}, u32[]{:S(2)}) collective-permute-start(bf16[32,1,16,320]{3,2,1,0:T(8,128)(2,1)S(1)} %copy.143), channel_id=1, source_target_pairs={{0,1},{1,2},{2,3},{3,4},{4,5},{5,6},{6,7},{7,8},{8,9},{9,10},{10,1... | collective-permute-start | bytes 983048 | tf_op jit(solution)/shard_map/ppermute | solution.py:18
  504.9 16.7 %collective-permute-start.3 = (bf16[32,1,16,320]{3,2,1,0:T(8,128)(2,1)}, bf16[32,1,16,320]{3,2,1,0:T(8,128)(2,1)}, u32[]{:S(2)}, u32[]{:S(2)}) collective-permute-start(bf16[32,1,16,320]{3,2,1,0:T(8,128)(2,1)} %copy.147), channel_id=1, source_target_pairs={{1,0},{2,1},{3,2},{4,3},{5,4},{6,5},{7,6},{8,7},{9,8},{10,9},{11,1... | collective-permute-start | bytes 983048 | tf_op jit(solution)/shard_map/ppermute | solution.py:19
  551.9 12.2 %copy-start.5 = (f32[8,16,320,2]{2,3,1,0:T(2,128)S(1)}, f32[8,16,320,2]{2,3,1,0:T(2,128)}, u32[]{:S(2)}) copy-start(f32[8,16,320,2]{2,3,1,0:T(2,128)} %fusion.56) | copy-start | bytes 983044
  551.9 12.2 %copy-start.7 = (f32[8,16,320]{2,1,0:T(8,128)S(1)}, f32[8,16,320]{2,1,0:T(8,128)}, u32[]{:S(2)}) copy-start(f32[8,16,320]{2,1,0:T(8,128)} %copy-done.6) | copy-start | bytes 491524
  551.9 12.2 %copy-start.9 = (f32[8,16,320]{2,1,0:T(8,128)S(1)}, f32[8,16,320]{2,1,0:T(8,128)}, u32[]{:S(2)}) copy-start(f32[8,16,320]{2,1,0:T(8,128)} %copy-done.8) | copy-start | bytes 491524
where the time goes:
time: 576 us; the launch traced here: 565 us
  blocking collectives  236 us (41%)
  matrix products  115 us (20%)
  local copies, waits for them, and re-layouts  85.2 us (15%)
  waiting for transfers between devices  58.7 us (10%)
  other arithmetic  52.1 us (9%)
  starting transfers between devices  17.3 us (3%)
    all_to_all x2, blocking collectives, body(): lax.all_to_all(back_z, 'slab', split_axis=2, concat_axis=3, tiled=True)  160 us
    all_to_all x1, blocking collectives, body(): lax.all_to_all(hybrid, 'slab', split_axis=3, concat_axis=2, tiled=True)  75.9 us
    all_to_all x1, waiting for transfers between devices, body(): lax.all_to_all(hybrid, 'slab', split_axis=3, concat_axis=2, tiled=True)  58.7 us
    concatenate x2, other arithmetic, padded_2(): array = jnp.concatenate([before, array, after], axis=dim)  36.8 us
    dot_general x4, matrix products, denoise(): jnp.einsum('oi,izxy->ozxy', conv_depth[:, offset, :], padded[:, offset:of...  35.5 us
    conv_general_dilated x2, matrix products, plane_conv(): lax.conv_general_dilated(values, conv_plane, (1, 1), 'SAME', dimension_nu...  26 us
    dot_general x2, matrix products, denoise(): jnp.einsum('pi,izxy->pzxy', conv_output, act_two, preferred_element_type=...  25.1 us
    slice x4, local copies, waits for them, and re-layouts, padded_2(): last = lax.slice_in_dim(array, length - width, length, axis=dim)  22.8 us
  transfers between devices with their start and end apart: 5, of which 1 were waited for; matrix products, arithmetic and copies ran while one was open for 7% of the time, Pallas kernels for 0%

commit v1 on v0

--- a/solution.py
+++ b/solution.py
@@ -85,22 +85,21 @@
 
 
 def denoise(noisy_low, conv_plane, conv_depth, conv_output):
-    act_one = plane_conv(noisy_low, conv_plane)
-    padded = padded_2(act_one, (("slab", 1),), 1)
     planes = noisy_low.shape[1]
-    mixed = jnp.einsum(
-        "oi,izxy->ozxy",
-        conv_depth[:, 0, :],
-        padded[:, 0:planes],
+    wide = padded_2(noisy_low, (("slab", 2),), 1)
+    first = lax.conv_general_dilated(
+        wide,
+        conv_plane,
+        (1, 1),
+        ((0, 0), (1, 1)),
+        dimension_numbers=("CNHW", "OIHW", "CNHW"),
         preferred_element_type=jnp.float32,
     )
-    for offset in range(1, 3):
-        mixed = mixed + jnp.einsum(
-            "oi,izxy->ozxy",
-            conv_depth[:, offset, :],
-            padded[:, offset : offset + planes],
-            preferred_element_type=jnp.float32,
-        )
+    act_one = jax.nn.relu(first).astype(jnp.bfloat16)
+    padded = jnp.pad(act_one, ((0, 0), (1, 1), (0, 0), (0, 0)))
+    stacked = jnp.concatenate([padded[:, t : t + planes] for t in range(3)], axis=0)
+    depth = conv_depth.reshape(conv_depth.shape[0], -1)
+    mixed = jnp.einsum("oi,izxy->ozxy", depth, stacked, preferred_element_type=jnp.float32)
     act_two = jax.nn.relu(mixed).astype(jnp.bfloat16)
     return jnp.einsum("pi,izxy->pzxy", conv_output, act_two, preferred_element_type=jnp.float32)
 
@@ -109,21 +108,26 @@
     table_y = dft_table(measured.shape[4])
     table_z = dft_table(measured.shape[2])
     sample_gate = line_mask.astype(jnp.float32)[:, None, :]
-    estimate = start_image
+    sent = jnp.concatenate([coil_maps, start_image.astype(jnp.bfloat16)[:, None]], axis=1)
+    got = lax.all_to_all(sent, "slab", split_axis=3, concat_axis=2, tiled=True)
+    coils = coil_maps.shape[1]
+    maps = got[:, :coils]
+    estimate = got[:, coils].astype(jnp.float32)
     for index_pass in range(PASSES):
         image_low = estimate.astype(jnp.bfloat16)
-        coil_image = complex_times(coil_maps, image_low[:, None])
+        coil_image = complex_times(maps, image_low[:, None])
         hybrid = forward_y(table_y, coil_image)
-        hybrid_read = lax.all_to_all(hybrid, "slab", split_axis=3, concat_axis=2, tiled=True)
-        back_z = residual_back(table_z, hybrid_read, measured, sample_gate)
-        back_local = lax.all_to_all(back_z, "slab", split_axis=2, concat_axis=3, tiled=True)
-        back_y = inverse_y(table_y, back_local)
-        gradient = conj_summed(coil_maps, back_y)
+        back_z = residual_back(table_z, hybrid, measured, sample_gate)
+        back_y = inverse_y(table_y, back_z)
+        gradient = conj_summed(maps, back_y)
         noisy_image = estimate - gradient
         estimate = noisy_image + denoise(
             noisy_image.astype(jnp.bfloat16), conv_plane, conv_depth, conv_output
         )
-    return estimate
+    out = lax.all_to_all(
+        estimate.astype(jnp.bfloat16), "slab", split_axis=1, concat_axis=2, tiled=True
+    )
+    return out.astype(jnp.float32)
 
 
 def solution(mesh):

time: 576 us -> 183 us (0.32); the launches traced: 565 us -> 183 us
  blocking collectives: 236 us -> 28.4 us
  matrix products: 115 us -> 39.4 us
  local copies, waits for them, and re-layouts: 85.2 us -> 18.3 us
  other arithmetic: 52.1 us -> 17.1 us
    all_to_all x3 -> x1, blocking collectives: 236 us -> 28.4 us  [body(): lax.all_to_all(estimate.astype(jnp.bfloat16), 'slab', split_axis=1, conca...]
    concatenate x2 -> x1, other arithmetic: 36.8 us -> 0.06 us  [padded_2(): array = jnp.concatenate([before, array, after], axis=dim)]
    dot_general x4 -> x0, matrix products: 35.5 us -> none  [denoise(): jnp.einsum('oi,izxy->ozxy', conv_depth[:, offset, :], padded[:, offset:of...]
    convert_element_type x6 -> x4, local copies, waits for them, and re-layouts: 31.5 us -> 1.23 us  [the longest x1 0.82 us: body(): return out.astype(jnp.float32)]
    conv_general_dilated x2, matrix products: 26 us -> 3.73 us  [denoise(): lax.conv_general_dilated(wide, conv_plane, (1, 1), ((0, 0), (1, 1)), dime...]
    slice x6 -> x4, local copies, waits for them, and re-layouts: 30.7 us -> 8.95 us  [the longest x2 7.39 us: denoise(): padded[:, t:t + planes]]
    ppermute x4 -> x0, local copies, waits for them, and re-layouts: 21.2 us -> none  [the longest x2 11 us: padded_2(): after = lax.ppermute(initial, axis, down)]
    dot_general x2, matrix products: 25.1 us -> 8.83 us  [denoise(): jnp.einsum('pi,izxy->pzxy', conv_output, act_two, preferred_element_type=...]
  transfers between devices with their start and end apart: 5 -> 5, of which waited for: 1 -> 3; matrix products, arithmetic and copies ran while one was open for 7% -> 4% of each run, Pallas kernels for 0% -> 0%
where the time goes in v1:
time: 183 us
  waiting for transfers between devices  56.9 us (31%)
  matrix products  39.4 us (22%)
  blocking collectives  28.4 us (16%)
  starting transfers between devices  22.4 us (12%)
  local copies, waits for them, and re-layouts  18.3 us (10%)
  other arithmetic  17.1 us (9%)
    all_to_all x1, waiting for transfers between devices, body(): got = lax.all_to_all(sent, 'slab', split_axis=3, concat_axis=2, tiled=True)  55.5 us
    all_to_all x1, blocking collectives, body(): lax.all_to_all(estimate.astype(jnp.bfloat16), 'slab', split_axis=1, conca...  28.4 us
    ppermute x2, starting transfers between devices, padded_2(): before = lax.ppermute(last, axis, up)  12.3 us
    dot_general x2, matrix products, residual_back(): jnp.einsum('qkpn,qckxy->pcnxy', table_z, residual, preferred_element_type...  11.5 us
    dot_general x2, matrix products, denoise(): jnp.einsum('pi,izxy->pzxy', conv_output, act_two, preferred_element_type=...  8.83 us
    dot_general x2, matrix products, inverse_y(): jnp.einsum('qkpn,qcabk->pcabn', table_y, back_z, preferred_element_type=j...  8.41 us
    all_to_all x1, starting transfers between devices, body(): got = lax.all_to_all(sent, 'slab', split_axis=3, concat_axis=2, tiled=True)  7.52 us
    unnamed x30, local copies, waits for them, and re-layouts  7.48 us
  transfers between devices with their start and end apart: 5, of which 3 were waited for; matrix products, arithmetic and copies ran while one was open for 4% of the time, Pallas kernels for 0%

profile of v1, /device:TPU:0, one launch (start us, length us, event | category | flops | bytes accessed | tf_op | source)
XLA Modules:
  0.0 182.8 jit_solution(14878563086047564175)
XLA Ops:
  0.0 1.1 copy.137
  1.1 2.7 %copy.50 = bf16[2,16,8,16,320]{4,2,1,0,3:T(8,128)(2,1)S(1)} copy(bf16[2,16,8,16,320]{4,3,2,1,0:T(8,128)(2,1)} %param.8) | data formatting | bytes 5242880 | tf_op args[1]
  3.8 2.3 %pad_maximum_fusion = bf16[2,17,8,16,320]{4,2,1,0,3:T(8,128)(2,1)} fusion(bf16[2,1,8,16,320]{4,2,1,0,3:T(8,128)(2,1)S(1)} %bitcast.282, bf16[2,16,8,16,320]{4,2,1,0,3:T(8,128)(2,1)S(1)} %copy.50), kind=kLoop, calls=%fused_computation.46 | loop fusion | flops 1392640 | bytes 5570560 | tf_op jit(solution)/shard_map/concatenate | solution.py:111
  6.1 7.5 %all-to-all-start = ((bf16[2,17,8,16,320]{4,2,1,0,3:T(8,128)(2,1)}), bf16[2,17,8,16,320]{4,2,1,0,3:T(8,128)(2,1)S(1)}, u32[]{:S(2)}, u32[]{:S(2)}) async-start(bf16[2,17,8,16,320]{4,2,1,0,3:T(8,128)(2,1)} %pad_maximum_fusion), calls=%async_computation | async-start | bytes 6684672 | tf_op jit(solution)/shard_map/all_to_all | solution.py:112
  13.6 0.7 convert_element_type.310
  14.3 0.3 fusion.121
  14.6 0.3 negate_convert_fusion.1
  14.9 0.7 pad_maximum_fusion.2
  15.6 2.0 %fusion.96 = bf16[320,1,320]{2,0,1:T(8,128)(2,1)S(1)} fusion(), kind=kLoop, calls=%fused_computation.121 | loop fusion | flops 1126400 | bytes 204800 | tf_op jit(solution)/shard_map/convert.28
  17.5 2.2 %negate_convert_fusion = (bf16[320,1,320]{2,0,1:T(8,128)(2,1)S(1)}, bf16[320,1,320]{2,0,1:T(8,128)(2,1)S(1)}) fusion(), kind=kLoop, calls=%fused_computation.114 | loop fusion | flops 1433600 | bytes 409600 | tf_op jit(solution)/shard_map/convert.24
  19.7 1.2 maximum_bitcast_fusion.16
  20.9 55.5 %all-to-all-done = bf16[2,17,8,16,320]{4,2,1,0,3:T(8,128)(2,1)S(1)} async-done(((bf16[2,17,8,16,320]{4,2,1,0,3:T(8,128)(2,1)}), bf16[2,17,8,16,320]{4,2,1,0,3:T(8,128)(2,1)S(1)}, u32[]{:S(2)}, u32[]{:S(2)}) %all-to-all-start) | async-done | bytes 2785312 | tf_op jit(solution)/shard_map/all_to_all | solution.py:112
  76.4 0.6 copy_bitcast_fusion
  77.1 1.5 fusion.134
  78.6 0.2 copy.99
  78.8 0.8 convert_bitcast_fusion
  79.5 0.9 copy.101
  80.7 1.9 %copy.100 = bf16[1,16,128,1,320]{2,4,1,3,0:T(8,128)(2,1)S(1)} copy(bf16[1,16,128,1,320]{4,2,1,0,3:T(8,128)(2,1)} %get-tuple-element.14) | data formatting | bytes 2621440
  82.6 0.8 fusion.82
  83.4 0.2 copy-done.3
  83.7 3.5 %fusion.54 = bf16[16,128,2,320,1]{1,3,4,2,0:T(8,128)(2,1)} fusion(bf16[1,16,128,320]{2,3,0,1:T(8,128)(2,1)S(1)} %get-tuple-element.18, bf16[1,16,128,320]{2,3,0,1:T(8,128)(2,1)S(1)} %get-tuple-element.17, bf16[1,320,2,320]{3,1,2,0:T(8,128)(2,1)S(1)} %copy-done.5, bf16[1,320,2,320]{3,1,2,0:T(8,128)(2,1)S(1)} %copy-done.3), kind=kOutput, calls=%fused_computation.81 | convolution fusion | flops 1684602880 | bytes 6062080 | tf_op jit(solution)/shard_map/pkqn,qcabn->pcabk/dot_general | solution.py:58
  87.2 5.7 %fusion.36 = bf16[16,320,2,128,1]{3,1,4,2,0:T(8,128)(2,1)} fusion(f32[128,320]{0,1:T(8,128)S(1)} %copy-done.8, bf16[16,128,2,320,1]{1,3,4,2,0:T(8,128)(2,1)} %fusion.54, bf16[2,16,128,1,320]{2,4,3,1,0:T(8,128)(2,1)} %param.7, bf16[2,128,2,128]{3,1,2,0:T(8,128)(2,1)S(1)} %copy-done.9), kind=kOutput, calls=%fused_computation.63 | convolution fusion | flops 1347420160 | bytes 8159232 | tf_op jit(solution)/shard_map/qkpn,qckxy->pcnxy/dot_general | solution.py:70
  92.9 4.3 %fusion.66 = f32[2,16,128,1,320]{2,4,1,3,0:T(8,128)S(1)} fusion(bf16[16,320,2,128,1]{3,1,4,2,0:T(8,128)(2,1)} %fusion.36, bf16[1,320,2,320]{3,1,2,0:T(8,128)(2,1)} %get-tuple-element.24, bf16[1,320,2,320]{3,1,2,0:T(8,128)(2,1)} %get-tuple-element.23), kind=kOutput, calls=%fused_computation.92 | convolution fusion | flops 1678131200 | bytes 8683520 | tf_op jit(solution)/shard_map/qkpn,qcabk->pcabn/dot_general | solution.py:64
  97.2 0.9 fusion.43
  98.2 1.1 fusion.99
  99.3 1.3 collective-permute-start.1
  100.6 4.0 %collective-permute-start = (bf16[2,128,1,320]{1,0,3,2:T(2,128)(2,1)}, bf16[2,128,1,320]{1,0,3,2:T(2,128)(2,1)}, u32[]{:S(2)}, u32[]{:S(2)}) collective-permute-start(bf16[2,128,1,320]{1,0,3,2:T(2,128)(2,1)} %fusion.99), channel_id=1, source_target_pairs={{0,1},{1,2},{2,3},{3,4},{4,5},{5,6},{6,7},{7,8},{8,9},{9,10},{10,1... | collective-permute-start | bytes 491528 | tf_op jit(solution)/shard_map/ppermute | solution.py:18
  104.7 0.6 collective-permute-done
  105.3 2.4 %maximum_convert_fusion.3 = bf16[32,128,1,320]{1,0,3,2:T(8,128)(2,1)S(1)} fusion(bf16[32,2,3,3]{0,1,3,2:T(2,128)(2,1)S(1)} %copy-done, bf16[2,128,1,320]{1,0,3,2:T(2,128)(2,1)S(1)} %collective-permute-done.1, bf16[2,128,1,320]{1,0,3,2:T(2,128)(2,1)} %fusion.99, bf16[2,128,1,320]{1,0,3,2:T(2,128)(2,1)} %collective-permute-done), kind=kOutput, calls=%fused_computation.45 | convolution fusion | flops 51183616 | bytes 3114112 | tf_op jit(solution)/shard_map/conv_general_dilated | solution.py:90
  107.7 3.7 %pad_slice_fusion.3 = (bf16[32,128,1,320]{1,0,3,2:T(8,128)(2,1)}, bf16[32,128,1,320]{1,0,3,2:T(8,128)(2,1)}) fusion(bf16[32,128,1,320]{1,0,3,2:T(8,128)(2,1)S(1)} %maximum_convert_fusion.3), kind=kLoop, calls=%fused_computation.33 | loop fusion | bytes 7864320 | tf_op jit(solution)/shard_map/slice | solution.py:100
  111.4 4.8 %fusion.15 = f32[128,320,2]{0,2,1:T(2,128)} fusion(bf16[32,96,1]{1,0,2:T(8,128)(2,1)S(1)} %reshape.582, bf16[32,128,1,320]{1,0,3,2:T(8,128)(2,1)} %get-tuple-element.22, bf16[32,128,1,320]{1,0,3,2:T(8,128)(2,1)} %copy-done.1, bf16[32,128,1,320]{1,0,3,2:T(8,128)(2,1)} %get-tuple-element.21, bf16[2,32]{1,0:T(2,128)(2,1)S(1)} %copy-done.11), kind=kOutput, calls=%fused_computation.49 | convolution fusion | flops 283115520 | bytes 8198272 | tf_op jit(solution)/shard_map/pi,izxy->pzxy/dot_general | solution.py:104
  116.2 1.0 fusion.132
  117.3 0.8 fusion.80
  118.1 0.2 copy-done.4
  118.4 3.5 %fusion.57 = bf16[16,128,2,320,1]{1,3,4,2,0:T(8,128)(2,1)} fusion(bf16[1,320,2,320]{3,1,2,0:T(8,128)(2,1)S(1)} %copy-done.6, bf16[1,320,2,320]{3,1,2,0:T(8,128)(2,1)S(1)} %copy-done.4, bf16[1,16,128,320]{2,3,1,0:T(8,128)(2,1)S(1)} %get-tuple-element.16, bf16[1,16,128,320]{2,3,1,0:T(8,128)(2,1)S(1)} %get-tuple-element.15), kind=kOutput, calls=%fused_computation.85 | convolution fusion | flops 1680670720 | bytes 6062080 | tf_op jit(solution)/shard_map/pkqn,qcabn->pcabk/dot_general | solution.py:58
  121.9 5.8 %fusion.33 = bf16[16,320,2,128,1]{3,1,4,2,0:T(8,128)(2,1)} fusion(f32[128,320]{0,1:T(8,128)} %convert_element_type.310, bf16[16,128,2,320,1]{1,3,4,2,0:T(8,128)(2,1)} %fusion.57, bf16[2,16,128,1,320]{2,4,3,1,0:T(8,128)(2,1)} %param.7, bf16[2,128,2,128]{3,1,2,0:T(8,128)(2,1)} %pad_maximum_fusion.2), kind=kOutput, calls=%fused_computation.61 | convolution fusion | flops 1347420160 | bytes 8159232 | tf_op jit(solution)/shard_map/qkpn,qckxy->pcnxy/dot_general | solution.py:70
  127.7 4.1 %fusion.63 = f32[2,16,128,1,320]{2,4,1,3,0:T(8,128)S(1)} fusion(bf16[16,320,2,128,1]{3,1,4,2,0:T(8,128)(2,1)} %fusion.33, bf16[1,320,2,320]{3,1,2,0:T(8,128)(2,1)} %get-tuple-element.24, bf16[1,320,2,320]{3,1,2,0:T(8,128)(2,1)S(1)} %copy-done.4), kind=kOutput, calls=%fused_computation.91 | convolution fusion | flops 1678131200 | bytes 8683520 | tf_op jit(solution)/shard_map/qkpn,qcabk->pcabn/dot_general | solution.py:64
  131.8 0.9 fusion.51
  132.7 1.3 collective-permute-start.3
  134.0 8.4 %collective-permute-start.2 = (bf16[2,128,1,320]{1,3,0,2:T(8,128)(2,1)S(1)}, bf16[2,128,1,320]{1,3,0,2:T(8,128)(2,1)S(1)}, u32[]{:S(2)}, u32[]{:S(2)}) collective-permute-start(bf16[2,128,1,320]{1,3,0,2:T(8,128)(2,1)S(1)} %convert_bitcast_fusion.3), channel_id=1, source_target_pairs={{0,1},{1,2},{2,3},{3,4},{4,5},{5,6},{6,7},{7,8},{8,9},{9,10},{10,1... | collective-permute-start | bytes 491528 | tf_op jit(solution)/shard_map/ppermute | solution.py:18
  142.4 0.8 collective-permute-done.2
  143.2 1.4 maximum_convert_fusion.1
  144.6 3.7 %pad_slice_fusion.1 = (bf16[32,128,1,320]{1,0,3,2:T(8,128)(2,1)}, bf16[32,128,1,320]{1,0,3,2:T(8,128)(2,1)}) fusion(bf16[32,128,1,320]{1,0,3,2:T(8,128)(2,1)S(1)} %maximum_convert_fusion.1), kind=kLoop, calls=%fused_computation.31 | loop fusion | bytes 7864320 | tf_op jit(solution)/shard_map/slice | solution.py:100
  148.3 4.0 %fusion.18 = f32[128,320,2]{0,2,1:T(2,128)} fusion(bf16[32,96,1]{1,0,2:T(8,128)(2,1)S(1)} %reshape.582, bf16[32,128,1,320]{1,0,3,2:T(8,128)(2,1)} %get-tuple-element.20, bf16[32,128,1,320]{1,0,3,2:T(8,128)(2,1)S(1)} %maximum_convert_fusion.1, bf16[32,128,1,320]{1,0,3,2:T(8,128)(2,1)} %get-tuple-element.19, bf16[2,32]{1,0:T(2,128)(2,1)S(1)} %copy-done.11), kind=kOutput, calls=%fused_computation.51 | convolution fusion | flops 283115520 | bytes 8198272 | tf_op jit(solution)/shard_map/pi,izxy->pzxy/dot_general | solution.py:104
  152.3 1.0 fusion.102
  153.4 0.2 copy.72
  153.6 28.4 %all_to_all.27 = bf16[2,128,1,320]{3,0,2,1:T(2,128)(2,1)S(1)} all-to-all(bf16[2,128,1,320]{3,0,2,1:T(2,128)(2,1)S(1)} %copy.72), channel_id=1, replica_groups=mesh['exam'=2,'slab'=16] {'slab'}, dimensions={1} | all-to-all | bytes 327680 | tf_op jit(solution)/shard_map/all_to_all | solution.py:127
  182.0 0.8 copy.74
  (35 shorter events, 0.9 us)
Async XLA Ops:
  0.0 105.3 %copy-start = (bf16[32,2,3,3]{0,1,3,2:T(2,128)(2,1)S(1)}, bf16[32,2,3,3]{0,1,3,2:T(2,128)(2,1)}, u32[]{:S(2)}) copy-start(bf16[32,2,3,3]{0,1,3,2:T(2,128)(2,1)} %param.11) | copy-start | bytes 3460
  6.1 7.5 %copy-start.7 = (s32[128,320]{0,1:T(8,128)S(1)}, s32[128,320]{0,1:T(8,128)}, u32[]{:S(2)}) copy-start(s32[128,320]{0,1:T(8,128)} %param.10) | copy-start | bytes 491524
  6.1 70.3 %all-to-all-start = ((bf16[2,17,8,16,320]{4,2,1,0,3:T(8,128)(2,1)}), bf16[2,17,8,16,320]{4,2,1,0,3:T(8,128)(2,1)S(1)}, u32[]{:S(2)}, u32[]{:S(2)}) async-start(bf16[2,17,8,16,320]{4,2,1,0,3:T(8,128)(2,1)} %pad_maximum_fusion), calls=%async_computation | async-start | bytes 6684672 | tf_op jit(solution)/shard_map/all_to_all | solution.py:112
  82.5 1.0 copy-start.3
  82.5 1.2 copy-start.5
  83.7 3.5 %copy-start.8 = (f32[128,320]{0,1:T(8,128)S(1)}, f32[128,320]{0,1:T(8,128)}, u32[]{:S(2)}) copy-start(f32[128,320]{0,1:T(8,128)} %convert_element_type.310) | copy-start | bytes 491524
  83.7 3.5 %copy-start.9 = (bf16[2,128,2,128]{3,1,2,0:T(8,128)(2,1)S(1)}, bf16[2,128,2,128]{3,1,2,0:T(8,128)(2,1)}, u32[]{:S(2)}) copy-start(bf16[2,128,2,128]{3,1,2,0:T(8,128)(2,1)} %pad_maximum_fusion.2) | copy-start | bytes 393220
  97.2 1.0 copy-start.2
  97.2 7.4 %copy-start.10 = (bf16[32,3,32]{2,0,1:T(8,128)(2,1)S(1)}, bf16[32,3,32]{2,0,1:T(8,128)(2,1)}, u32[]{:S(2)}) copy-start(bf16[32,3,32]{2,0,1:T(8,128)(2,1)} %param.12) | copy-start | bytes 18436
  99.3 5.4 %collective-permute-start.1 = (bf16[2,128,1,320]{1,0,3,2:T(2,128)(2,1)}, bf16[2,128,1,320]{1,0,3,2:T(2,128)(2,1)S(1)}, u32[]{:S(2)}, u32[]{:S(2)}) collective-permute-start(bf16[2,128,1,320]{1,0,3,2:T(2,128)(2,1)} %fusion.99), channel_id=1, source_target_pairs={{1,0},{2,1},{3,2},{4,3},{5,4},{6,5},{7,6},{8,7},{9,8},{10,9},{11,1... | collective-permute-start | bytes 491528 | tf_op jit(solution)/shard_map/ppermute | solution.py:19
  100.6 4.7 %collective-permute-start = (bf16[2,128,1,320]{1,0,3,2:T(2,128)(2,1)}, bf16[2,128,1,320]{1,0,3,2:T(2,128)(2,1)}, u32[]{:S(2)}, u32[]{:S(2)}) collective-permute-start(bf16[2,128,1,320]{1,0,3,2:T(2,128)(2,1)} %fusion.99), channel_id=1, source_target_pairs={{0,1},{1,2},{2,3},{3,4},{4,5},{5,6},{6,7},{7,8},{8,9},{9,10},{10,1... | collective-permute-start | bytes 491528 | tf_op jit(solution)/shard_map/ppermute | solution.py:18
  107.7 3.7 %copy-start.1 = (bf16[32,128,1,320]{1,0,3,2:T(8,128)(2,1)}, bf16[32,128,1,320]{1,0,3,2:T(8,128)(2,1)S(1)}, u32[]{:S(2)}) copy-start(bf16[32,128,1,320]{1,0,3,2:T(8,128)(2,1)S(1)} %maximum_convert_fusion.3) | copy-start | bytes 7864324
  107.7 3.7 %copy-start.11 = (bf16[2,32]{1,0:T(2,128)(2,1)S(1)}, bf16[2,32]{1,0:T(2,128)(2,1)}, u32[]{:S(2)}) copy-start(bf16[2,32]{1,0:T(2,128)(2,1)} %param.13) | copy-start | bytes 388
  117.2 1.0 copy-start.4
  117.3 1.2 copy-start.6
  132.7 9.7 %collective-permute-start.3 = (bf16[2,128,1,320]{1,3,0,2:T(8,128)(2,1)S(1)}, bf16[2,128,1,320]{1,3,0,2:T(8,128)(2,1)S(1)}, u32[]{:S(2)}, u32[]{:S(2)}) collective-permute-start(bf16[2,128,1,320]{1,3,0,2:T(8,128)(2,1)S(1)} %convert_bitcast_fusion.3), channel_id=1, source_target_pairs={{1,0},{2,1},{3,2},{4,3},{5,4},{6,5},{7,6},{8,7},{9,8},{10,9},{11,1... | collective-permute-start | bytes 491528 | tf_op jit(solution)/shard_map/ppermute | solution.py:19
  134.0 9.1 %collective-permute-start.2 = (bf16[2,128,1,320]{1,3,0,2:T(8,128)(2,1)S(1)}, bf16[2,128,1,320]{1,3,0,2:T(8,128)(2,1)S(1)}, u32[]{:S(2)}, u32[]{:S(2)}) collective-permute-start(bf16[2,128,1,320]{1,3,0,2:T(8,128)(2,1)S(1)} %convert_bitcast_fusion.3), channel_id=1, source_target_pairs={{0,1},{1,2},{2,3},{3,4},{4,5},{5,6},{6,7},{7,8},{8,9},{9,10},{10,1... | collective-permute-start | bytes 491528 | tf_op jit(solution)/shard_map/ppermute | solution.py:18

commit v2 on v1

--- a/solution.py
+++ b/solution.py
@@ -1,24 +1,118 @@
+import functools
 import math
 
 import jax
 import jax.numpy as jnp
 from jax import lax
+from jax.experimental import pallas as pl
+from jax.experimental.pallas import tpu as pltpu
 from jax.sharding import PartitionSpec as P
 
 PASSES = 2
 
 
-def padded_2(array, sides, width):
-    for axis, dim in sides:
-        size, length = (lax.axis_size(axis), array.shape[dim])
-        up = [(i, (i + 1) % size) for i in range(size - 1)]
-        down = [(j, i) for i, j in up]
-        last = lax.slice_in_dim(array, length - width, length, axis=dim)
-        initial = lax.slice_in_dim(array, 0, width, axis=dim)
-        before = lax.ppermute(last, axis, up)
-        after = lax.ppermute(initial, axis, down)
-        array = jnp.concatenate([before, array, after], axis=dim)
-    return array
+def partner(me, flips):
+    other = me
+    bit = 1
+    while bit <= flips:
+        if flips & bit:
+            other = other + bit * (1 - 2 * lax.rem(lax.div(me, bit), 2))
+        bit *= 2
+    return other
+
+
+def flip_order(size):
+    half = size // 2
+    order = []
+    for low in range(half):
+        order.append(half + low)
+        if low:
+            order.append(low)
+    return order
+
+
+def exchange_kernel(size, sent_ref, got_ref, send_sem, recv_sem, own_sem):
+    me = lax.axis_index("slab")
+    order = flip_order(size)
+    barrier = pltpu.get_barrier_semaphore()
+    for flips in order:
+        pl.semaphore_signal(barrier, inc=1, device_id={"slab": partner(me, flips)})
+    own = pltpu.make_async_copy(sent_ref.at[me], got_ref.at[me], own_sem)
+    own.start()
+    pl.semaphore_wait(barrier, size - 1)
+    copies = []
+    for flips in order:
+        to = partner(me, flips)
+        copy = pltpu.make_async_remote_copy(
+            src_ref=sent_ref.at[to],
+            dst_ref=got_ref.at[me],
+            send_sem=send_sem.at[flips],
+            recv_sem=recv_sem.at[flips],
+            device_id={"slab": to},
+        )
+        copy.start()
+        copies.append(copy)
+    own.wait()
+    for copy in copies:
+        copy.wait()
+
+
+def exchange(blocks, identity, space):
+    size = blocks.shape[0]
+    return pl.pallas_call(
+        functools.partial(exchange_kernel, size),
+        out_shape=jax.ShapeDtypeStruct(blocks.shape, blocks.dtype),
+        in_specs=[pl.BlockSpec(memory_space=space)],
+        out_specs=pl.BlockSpec(memory_space=space),
+        scratch_shapes=[
+            pltpu.SemaphoreType.DMA((size,)),
+            pltpu.SemaphoreType.DMA((size,)),
+            pltpu.SemaphoreType.DMA,
+        ],
+        compiler_params=pltpu.CompilerParams(
+            collective_id=identity, has_side_effects=True, vmem_limit_bytes=32 << 20
+        ),
+    )(blocks)
+
+
+def halo_kernel(size, plane_ref, out_ref, send_sem, recv_sem):
+    me = lax.axis_index("slab")
+    sides = (lax.rem(me + 1, size), lax.rem(me + size - 1, size))
+    barrier = pltpu.get_barrier_semaphore()
+    for side in sides:
+        pl.semaphore_signal(barrier, inc=1, device_id={"slab": side})
+    pl.semaphore_wait(barrier, 2)
+    copies = []
+    for at, side in enumerate(sides):
+        copy = pltpu.make_async_remote_copy(
+            src_ref=plane_ref,
+            dst_ref=out_ref.at[at],
+            send_sem=send_sem.at[at],
+            recv_sem=recv_sem.at[at],
+            device_id={"slab": side},
+        )
+        copy.start()
+        copies.append(copy)
+    for copy in copies:
+        copy.wait()
+
+
+def halos(plane, identity):
+    size = lax.axis_size("slab")
+    me = lax.axis_index("slab")
+    got = pl.pallas_call(
+        functools.partial(halo_kernel, size),
+        out_shape=jax.ShapeDtypeStruct((2,) + plane.shape, plane.dtype),
+        in_specs=[pl.BlockSpec(memory_space=pltpu.VMEM)],
+        out_specs=pl.BlockSpec(memory_space=pltpu.VMEM),
+        scratch_shapes=[pltpu.SemaphoreType.DMA((2,)), pltpu.SemaphoreType.DMA((2,))],
+        compiler_params=pltpu.CompilerParams(
+            collective_id=identity, has_side_effects=True, vmem_limit_bytes=16 << 20
+        ),
+    )(plane)
+    before = jnp.where(me == 0, jnp.zeros_like(plane), got[0])
+    after = jnp.where(me == size - 1, jnp.zeros_like(plane), got[1])
+    return before, after
 
 
 def dft_table(length):
@@ -84,9 +178,11 @@
     return jax.nn.relu(first).astype(jnp.bfloat16)
 
 
-def denoise(noisy_low, conv_plane, conv_depth, conv_output):
-    planes = noisy_low.shape[1]
-    wide = padded_2(noisy_low, (("slab", 2),), 1)
+def denoise(noisy_low, conv_plane, conv_depth, conv_output, identity):
+    parts, planes, reads, lines = noisy_low.shape
+    flat = noisy_low.reshape(parts, planes * reads, lines)
+    before, after = halos(flat[:, :, :], identity)
+    wide = jnp.stack([before, flat, after], axis=2).reshape(parts, planes, 3, lines)
     first = lax.conv_general_dilated(
         wide,
         conv_plane,
@@ -109,8 +205,11 @@
     table_z = dft_table(measured.shape[2])
     sample_gate = line_mask.astype(jnp.float32)[:, None, :]
     sent = jnp.concatenate([coil_maps, start_image.astype(jnp.bfloat16)[:, None]], axis=1)
-    got = lax.all_to_all(sent, "slab", split_axis=3, concat_axis=2, tiled=True)
-    coils = coil_maps.shape[1]
+    parts, coils, slices, reads, lines = coil_maps.shape
+    size = lax.axis_size("slab")
+    sent = jnp.moveaxis(sent, 3, 0).reshape(size, -1, lines)
+    got = exchange(sent, 1, pl.ANY).reshape(size, parts, coils + 1, slices, lines)
+    got = jnp.moveaxis(got, 0, 2).reshape(parts, coils + 1, size * slices, 1, lines)
     maps = got[:, :coils]
     estimate = got[:, coils].astype(jnp.float32)
     for index_pass in range(PASSES):
@@ -122,12 +221,12 @@
         gradient = conj_summed(maps, back_y)
         noisy_image = estimate - gradient
         estimate = noisy_image + denoise(
-            noisy_image.astype(jnp.bfloat16), conv_plane, conv_depth, conv_output
+            noisy_image.astype(jnp.bfloat16), conv_plane, conv_depth, conv_output, 3 + index_pass
         )
-    out = lax.all_to_all(
-        estimate.astype(jnp.bfloat16), "slab", split_axis=1, concat_axis=2, tiled=True
-    )
-    return out.astype(jnp.float32)
+    leave = estimate.astype(jnp.bfloat16).reshape(parts, size, slices, lines)
+    leave = jnp.moveaxis(leave, 1, 0).reshape(size, parts * slices, lines)
+    out = exchange(leave, 2, pltpu.VMEM).reshape(reads, parts, slices, lines)
+    return jnp.transpose(out, (1, 2, 0, 3)).astype(jnp.float32)
 
 
 def solution(mesh):

time: 183 us -> 178 us (0.973)
  Pallas kernels: 0 us -> 102 us
  waiting for transfers between devices: 56.9 us -> 0 us
  blocking collectives: 28.4 us -> 0 us
  starting transfers between devices: 22.4 us -> 0 us
    pallas_call x0 -> x4, Pallas kernels: none -> 102 us  [the longest x2 79.9 us: exchange(): pl.pallas_call(functools.partial(exchange_kernel, size), out_shape=jax.Sh...]
    all_to_all x1 -> x0, waiting for transfers between devices: 55.5 us -> none  [body(): got = lax.all_to_all(sent, 'slab', split_axis=3, concat_axis=2, tiled=True)]
    all_to_all x1 -> x0, blocking collectives: 28.4 us -> none  [body(): lax.all_to_all(estimate.astype(jnp.bfloat16), 'slab', split_axis=1, conca...]
    ppermute x4 -> x0, starting transfers between devices: 14.9 us -> none  [the longest x2 12.3 us: padded_2(): before = lax.ppermute(last, axis, up)]
    all_to_all x1 -> x0, starting transfers between devices: 7.52 us -> none  [body(): got = lax.all_to_all(sent, 'slab', split_axis=3, concat_axis=2, tiled=True)]
    unnamed x30 -> x31, local copies, waits for them, and re-layouts: 7.48 us -> 1.48 us
    another operation x0 -> x2, local copies, waits for them, and re-layouts: none -> 3.73 us  [denoise(): jnp.stack([before, flat, after], axis=2).reshape(parts, planes, 3, lines)]
    dot_general x0 -> x2, local copies, waits for them, and re-layouts: none -> 3.02 us  [denoise(): jnp.einsum('pi,izxy->pzxy', conv_output, act_two, preferred_element_type=...]
  transfers between devices with their start and end apart: 5 -> 0, of which waited for: 3 -> 0; matrix products, arithmetic and copies ran while one was open for 4% -> 0% of each run, Pallas kernels for 0% -> 0%
where the time goes in v2:
time: 178 us; the launch traced here: 177 us
  Pallas kernels  102 us (57%)
  matrix products  40.4 us (23%)
  local copies, waits for them, and re-layouts  17.9 us (10%)
  other arithmetic  16.5 us (9%)
    pallas_call x2, Pallas kernels, exchange(): pl.pallas_call(functools.partial(exchange_kernel, size), out_shape=jax.Sh...  79.9 us
    pallas_call x2, Pallas kernels, halos(): pl.pallas_call(functools.partial(halo_kernel, size), out_shape=jax.ShapeD...  22.1 us
    dot_general x2, matrix products, residual_back(): jnp.einsum('qkpn,qckxy->pcnxy', table_z, residual, preferred_element_type...  11.6 us
    dot_general x2, matrix products, inverse_y(): jnp.einsum('qkpn,qcabk->pcabn', table_y, back_z, preferred_element_type=j...  9.23 us
    dot_general x2, matrix products, denoise(): jnp.einsum('pi,izxy->pzxy', conv_output, act_two, preferred_element_type=...  8.93 us
    slice x2, local copies, waits for them, and re-layouts, denoise(): padded[:, t:t + planes]  7.39 us
    dot_general x2, matrix products, forward_y(): jnp.einsum('pkqn,qcabn->pcabk', table_y, coil_image, preferred_element_ty...  7.05 us
    another operation x4, other arithmetic  4.68 us

profile of v2, /device:TPU:0, one launch (start us, length us, event | category | flops | bytes accessed | tf_op | source)
XLA Modules:
  0.0 177.2 jit_solution(18185911732380830582)
XLA Ops:
  0.0 0.9 copy.82
  0.9 0.1 reshape.661
  1.0 0.3 fusion.113
  1.3 0.3 negate_convert_fusion.1
  1.6 0.7 pad_maximum_fusion.2
  2.3 0.9 convert_element_type.309
  3.2 1.1 convert_bitcast_fusion.4
  4.3 2.0 %fusion.87 = bf16[320,1,320]{2,0,1:T(8,128)(2,1)S(1)} fusion(), kind=kLoop, calls=%fused_computation.117 | loop fusion | flops 1126400 | bytes 204800 | tf_op jit(solution)/shard_map/convert.27
  6.2 2.2 %negate_convert_fusion = (bf16[320,1,320]{2,0,1:T(8,128)(2,1)S(1)}, bf16[320,1,320]{2,0,1:T(8,128)(2,1)S(1)}) fusion(), kind=kLoop, calls=%fused_computation.110 | loop fusion | flops 1433600 | bytes 409600 | tf_op jit(solution)/shard_map/convert.23
  8.4 0.2 maximum_bitcast_fusion.16
  8.7 0.6 maximum_bitcast_fusion.4
  9.2 0.7 copy.68
  10.0 61.6 %shard_map.73 = bf16[16,272,320]{2,1,0:T(8,128)(2,1)S(1)} custom-call(bf16[16,272,320]{2,1,0:T(8,128)(2,1)S(1)} %bitcast.377), custom_call_target="tpu_custom_call" | custom-call | tf_op jit(solution)/shard_map/pallas_call | solution.py:62
  71.6 0.6 copy.148
  72.2 0.6 fusion.79
  72.8 0.6 fusion.81
  73.5 3.5 %fusion.40 = bf16[16,128,2,320,1]{1,3,4,2,0:T(8,128)(2,1)} fusion(bf16[1,320,2,320]{3,1,2,0:T(8,128)(2,1)S(1)} %get-tuple-element.22, bf16[1,320,2,320]{3,1,2,0:T(8,128)(2,1)S(1)} %get-tuple-element.21, bf16[1,16,128,320]{3,2,1,0:T(8,128)(2,1)S(1)} %fusion.79, bf16[1,16,128,320]{3,2,1,0:T(8,128)(2,1)S(1)} %fusion.81), kind=kOutput, calls=%fused_computation.72 | convolution fusion | flops 1680670720 | bytes 6062080 | tf_op jit(solution)/shard_map/pkqn,qcabn->pcabk/dot_general | solution.py:152
  77.0 5.8 %fusion.62 = bf16[16,320,2,128,1]{3,1,4,2,0:T(8,128)(2,1)} fusion(f32[128,320]{0,1:T(8,128)S(1)} %convert_element_type.309, bf16[16,128,2,320,1]{1,3,4,2,0:T(8,128)(2,1)} %fusion.40, bf16[2,16,128,1,320]{2,4,3,1,0:T(8,128)(2,1)} %param.7, bf16[2,128,2,128]{3,1,2,0:T(8,128)(2,1)} %pad_maximum_fusion.2), kind=kOutput, calls=%fused_computation.89 | convolution fusion | flops 1347420160 | bytes 8159232 | tf_op jit(solution)/shard_map/qkpn,qckxy->pcnxy/dot_general | solution.py:164
  82.8 4.6 %convolution_bitcast_fusion.1 = f32[2,16,128,1,320]{4,2,0,3,1:T(8,128)S(1)} fusion(bf16[16,320,2,128,1]{3,1,4,2,0:T(8,128)(2,1)} %fusion.62, bf16[1,320,2,320]{3,1,2,0:T(8,128)(2,1)} %copy-done.6, bf16[1,320,2,320]{3,1,2,0:T(8,128)(2,1)} %copy-done.4), kind=kOutput, calls=%fused_computation.75 | convolution fusion | flops 1679360000 | bytes 8683520 | tf_op jit(solution)/shard_map/qkpn,qcabk->pcabn/dot_general | solution.py:158
  87.5 1.2 fusion.33
  88.7 0.1 fusion.90
  88.8 0.1 fusion.92.plane_ref
  88.8 7.9 %shard_map.74 = bf16[2,2,128,320]{3,2,1,0:T(8,128)(2,1)S(1)} custom-call(bf16[2,128,320]{2,1,0:T(8,128)(2,1)S(1)} %fusion.92.plane_ref), custom_call_target="tpu_custom_call" | custom-call | tf_op jit(solution)/shard_map/pallas_call | solution.py:103
  96.8 0.9 pad_maximum_fusion
  97.7 2.9 %copy.81 = bf16[2,128,3,320]{1,0,3,2:T(2,128)(2,1)} copy(bf16[2,128,3,320]{3,1,0,2:T(8,128)(2,1)} %pad_maximum_fusion) | data formatting | bytes 983040 | tf_op jit(solution)/shard_map/stack | solution.py:185
  100.6 2.3 %maximum_convert_fusion.3 = bf16[32,128,1,320]{1,0,3,2:T(8,128)(2,1)S(1)} fusion(bf16[2,128,3,320]{1,0,3,2:T(2,128)(2,1)} %copy.81, bf16[32,2,3,3]{0,1,3,2:T(2,128)(2,1)S(1)} %copy-done), kind=kOutput, calls=%fused_computation.45 | convolution fusion | flops 49709056 | bytes 3114112 | tf_op jit(solution)/shard_map/conv_general_dilated | solution.py:186
  102.9 3.7 %pad_slice_fusion.3 = (bf16[32,128,1,320]{1,0,3,2:T(8,128)(2,1)}, bf16[32,128,1,320]{1,0,3,2:T(8,128)(2,1)}) fusion(bf16[32,128,1,320]{1,0,3,2:T(8,128)(2,1)S(1)} %maximum_convert_fusion.3), kind=kLoop, calls=%fused_computation.29 | loop fusion | bytes 7864320 | tf_op jit(solution)/shard_map/slice | solution.py:196
  106.6 4.8 %fusion.43 = f32[128,320,2]{0,2,1:T(2,128)} fusion(bf16[32,96,1]{1,0,2:T(8,128)(2,1)S(1)} %reshape.661, bf16[32,128,1,320]{1,0,3,2:T(8,128)(2,1)} %get-tuple-element.16, bf16[32,128,1,320]{1,0,3,2:T(8,128)(2,1)} %copy-done.1, bf16[32,128,1,320]{1,0,3,2:T(8,128)(2,1)} %get-tuple-element.15, bf16[2,32]{1,0:T(2,128)(2,1)} %param.13), kind=kOutput, calls=%fused_computation.77 | convolution fusion | flops 283115520 | bytes 8198272 | tf_op jit(solution)/shard_map/pi,izxy->pzxy/dot_general | solution.py:200
  111.4 1.9 %copy.83 = f32[128,320,2]{1,0,2:T(8,128)} copy(f32[128,320,2]{0,2,1:T(2,128)} %fusion.43) | data formatting | bytes 655360 | tf_op jit(solution)/shard_map/pi,izxy->pzxy/dot_general | solution.py:200
  113.3 1.9 %fusion.122 = (bf16[2,128,320]{2,1,0:T(8,128)(2,1)S(1)}, f32[2,128,320]{2,1,0:T(8,128)}) fusion(f32[128,320,2]{1,0,2:T(8,128)} %copy.83, f32[1,128,320]{2,1,0:T(8,128)} %bitcast.394, f32[1,128,320]{2,1,0:T(8,128)S(1)} %bitcast.391, bf16[2,17,128,1,320]{4,2,0,3,1:T(8,128)(2,1)S(1)} %bitcast.385), kind=kLoop, calls=%fused_computation.172 | loop fusion | flops 409600 | bytes 1310720 | tf_op jit(solution)/shard_map/convert_element_type | solution.py:216
  115.2 0.6 fusion.78
  115.9 0.6 fusion.80
  116.5 0.4 copy-done.5
  116.9 0.1 copy-done.7
  117.0 3.5 %fusion.38 = bf16[16,128,2,320,1]{1,3,4,2,0:T(8,128)(2,1)} fusion(bf16[1,320,2,320]{3,1,2,0:T(8,128)(2,1)S(1)} %copy-done.7, bf16[1,320,2,320]{3,1,2,0:T(8,128)(2,1)S(1)} %copy-done.5, bf16[1,16,128,320]{3,2,1,0:T(8,128)(2,1)S(1)} %fusion.78, bf16[1,16,128,320]{3,2,1,0:T(8,128)(2,1)S(1)} %fusion.80), kind=kOutput, calls=%fused_computation.70 | convolution fusion | flops 1680670720 | bytes 6062080 | tf_op jit(solution)/shard_map/pkqn,qcabn->pcabk/dot_general | solution.py:152
  120.5 5.8 %fusion.59 = bf16[16,320,2,128,1]{3,1,4,2,0:T(8,128)(2,1)} fusion(f32[128,320]{0,1:T(8,128)S(1)} %copy-done.13, bf16[16,128,2,320,1]{1,3,4,2,0:T(8,128)(2,1)} %fusion.38, bf16[2,16,128,1,320]{2,4,3,1,0:T(8,128)(2,1)} %param.7, bf16[2,128,2,128]{3,1,2,0:T(8,128)(2,1)} %pad_maximum_fusion.2), kind=kOutput, calls=%fused_computation.87 | convolution fusion | flops 1347420160 | bytes 8159232 | tf_op jit(solution)/shard_map/qkpn,qckxy->pcnxy/dot_general | solution.py:164
  126.3 4.6 %convolution_bitcast_fusion = f32[2,16,128,1,320]{4,2,0,3,1:T(8,128)S(1)} fusion(bf16[16,320,2,128,1]{3,1,4,2,0:T(8,128)(2,1)} %fusion.59, bf16[1,320,2,320]{3,1,2,0:T(8,128)(2,1)} %copy-done.6, bf16[1,320,2,320]{3,1,2,0:T(8,128)(2,1)} %copy-done.4), kind=kOutput, calls=%fused_computation.74 | convolution fusion | flops 1679360000 | bytes 8683520 | tf_op jit(solution)/shard_map/qkpn,qcabk->pcabn/dot_general | solution.py:158
  130.9 1.2 fusion.37
  132.3 14.3 %shard_map.75 = bf16[2,2,128,320]{3,2,1,0:T(8,128)(2,1)S(1)} custom-call(bf16[2,128,320]{2,1,0:T(8,128)(2,1)S(1)} %fusion.102.plane_ref), custom_call_target="tpu_custom_call" | custom-call | tf_op jit(solution)/shard_map/pallas_call | solution.py:103
  146.6 0.1 pad_maximum_fusion.1
  146.8 0.8 copy.93
  147.6 1.3 maximum_convert_fusion.1
  148.9 3.7 %pad_slice_fusion.1 = (bf16[32,128,1,320]{1,0,3,2:T(8,128)(2,1)}, bf16[32,128,1,320]{1,0,3,2:T(8,128)(2,1)}) fusion(bf16[32,128,1,320]{1,0,3,2:T(8,128)(2,1)S(1)} %maximum_convert_fusion.1), kind=kLoop, calls=%fused_computation.27 | loop fusion | bytes 7864320 | tf_op jit(solution)/shard_map/slice | solution.py:196
  152.7 4.1 %fusion.46 = f32[128,320,2]{0,2,1:T(2,128)} fusion(bf16[32,96,1]{1,0,2:T(8,128)(2,1)S(1)} %reshape.661, bf16[32,128,1,320]{1,0,3,2:T(8,128)(2,1)} %get-tuple-element.14, bf16[32,128,1,320]{1,0,3,2:T(8,128)(2,1)S(1)} %maximum_convert_fusion.1, bf16[32,128,1,320]{1,0,3,2:T(8,128)(2,1)} %get-tuple-element.13, bf16[2,32]{1,0:T(2,128)(2,1)S(1)} %copy-done.14), kind=kOutput, calls=%fused_computation.79 | convolution fusion | flops 283115520 | bytes 8198272 | tf_op jit(solution)/shard_map/pi,izxy->pzxy/dot_general | solution.py:200
  156.8 1.1 copy.94
  157.9 0.1 copy_bitcast_fusion.2.sent_ref
  158.0 18.3 %shard_map.76 = bf16[16,16,320]{2,1,0:T(8,128)(2,1)S(1)} custom-call(bf16[16,16,320]{2,1,0:T(8,128)(2,1)S(1)} %copy_bitcast_fusion.2.sent_ref), custom_call_target="tpu_custom_call" | custom-call | tf_op jit(solution)/shard_map/pallas_call | solution.py:62
  176.3 0.9 copy.149
  (36 shorter events, 0.4 us)
Async XLA Ops:
  0.0 100.6 %copy-start = (bf16[32,2,3,3]{0,1,3,2:T(2,128)(2,1)S(1)}, bf16[32,2,3,3]{0,1,3,2:T(2,128)(2,1)}, u32[]{:S(2)}) copy-start(bf16[32,2,3,3]{0,1,3,2:T(2,128)(2,1)} %param.11) | copy-start | bytes 3460
  0.0 8.6 %copy-start.8 = (bf16[2,16,8,16,320]{4,3,2,1,0:T(8,128)(2,1)S(1)}, bf16[2,16,8,16,320]{4,3,2,1,0:T(8,128)(2,1)}, u32[]{:S(2)}) copy-start(bf16[2,16,8,16,320]{4,3,2,1,0:T(8,128)(2,1)} %param.8) | copy-start | bytes 7864324
  3.2 73.8 %copy-start.12 = (f32[128,320]{0,1:T(8,128)}, f32[128,320]{0,1:T(8,128)S(1)}, u32[]{:S(2)}) copy-start(f32[128,320]{0,1:T(8,128)S(1)} %convert_element_type.309) | copy-start | bytes 491524
  8.6 64.9 %copy-start.4 = (bf16[1,320,2,320]{3,1,2,0:T(8,128)(2,1)}, bf16[1,320,2,320]{3,1,2,0:T(8,128)(2,1)S(1)}, u32[]{:S(2)}) copy-start(bf16[1,320,2,320]{3,1,2,0:T(8,128)(2,1)S(1)} %get-tuple-element.21) | copy-start | bytes 1228804
  8.6 64.9 %copy-start.6 = (bf16[1,320,2,320]{3,1,2,0:T(8,128)(2,1)}, bf16[1,320,2,320]{3,1,2,0:T(8,128)(2,1)S(1)}, u32[]{:S(2)}) copy-start(bf16[1,320,2,320]{3,1,2,0:T(8,128)(2,1)S(1)} %get-tuple-element.22) | copy-start | bytes 1228804
  88.7 8.1 %copy-start.9 = (f32[128,320]{1,0:T(8,128)}, f32[128,320]{1,0:T(8,128)S(1)}, u32[]{:S(2)}) copy-start(f32[128,320]{1,0:T(8,128)S(1)} %get-tuple-element.8) | copy-start | bytes 491524
  102.9 3.7 %copy-start.1 = (bf16[32,128,1,320]{1,0,3,2:T(8,128)(2,1)}, bf16[32,128,1,320]{1,0,3,2:T(8,128)(2,1)S(1)}, u32[]{:S(2)}) copy-start(bf16[32,128,1,320]{1,0,3,2:T(8,128)(2,1)S(1)} %maximum_convert_fusion.3) | copy-start | bytes 7864324
  115.8 1.0 copy-start.5
  115.8 1.2 copy-start.7
  117.0 3.5 %copy-start.13 = (f32[128,320]{0,1:T(8,128)S(1)}, f32[128,320]{0,1:T(8,128)}, u32[]{:S(2)}) copy-start(f32[128,320]{0,1:T(8,128)} %copy-done.12) | copy-start | bytes 491524
  130.9 1.3 copy-start.2
  132.2 14.5 %copy-start.10 = (f32[128,320]{1,0:T(8,128)}, f32[128,320]{1,0:T(8,128)S(1)}, u32[]{:S(2)}) copy-start(f32[128,320]{1,0:T(8,128)S(1)} %get-tuple-element.6) | copy-start | bytes 491524
  148.9 3.7 %copy-start.14 = (bf16[2,32]{1,0:T(2,128)(2,1)S(1)}, bf16[2,32]{1,0:T(2,128)(2,1)}, u32[]{:S(2)}) copy-start(bf16[2,32]{1,0:T(2,128)(2,1)} %param.13) | copy-start | bytes 388
  152.7 5.3 %copy-start.3 = (f32[2,128,320]{2,1,0:T(8,128)S(1)}, f32[2,128,320]{2,1,0:T(8,128)}, u32[]{:S(2)}) copy-start(f32[2,128,320]{2,1,0:T(8,128)} %get-tuple-element.10) | copy-start | bytes 983044
  152.7 5.3 %copy-start.11 = (f32[128,320]{1,0:T(8,128)S(1)}, f32[128,320]{1,0:T(8,128)}, u32[]{:S(2)}) copy-start(f32[128,320]{1,0:T(8,128)} %copy-done.10) | copy-start | bytes 491524

commit v3 on v2

v3 whole, which is shorter than its diff:
```python
import functools
import math

import jax
import jax.numpy as jnp
import numpy as np
from jax import lax
from jax.experimental import pallas as pl
from jax.experimental.pallas import tpu as pltpu
from jax.sharding import PartitionSpec as P

PASSES = 2


def partner(me, flips):
    other = me
    bit = 1
    while bit <= flips:
        if flips & bit:
            other = other + bit * (1 - 2 * lax.rem(lax.div(me, bit), 2))
        bit *= 2
    return other


def flip_order(size):
    half = size // 2
    order = []
    for low in range(half):
        order.append(half + low)
        if low:
            order.append(low)
    return order


def exchange_kernel(size, sent_ref, got_ref, send_sem, recv_sem, own_sem):
    me = lax.axis_index("slab")
    order = flip_order(size)
    barrier = pltpu.get_barrier_semaphore()
    for flips in order:
        pl.semaphore_signal(barrier, inc=1, device_id={"slab": partner(me, flips)})
    own = pltpu.make_async_copy(sent_ref.at[me], got_ref.at[me], own_sem)
    own.start()
    pl.semaphore_wait(barrier, size - 1)
    copies = []
    for flips in order:
        to = partner(me, flips)
        copy = pltpu.make_async_remote_copy(
            src_ref=sent_ref.at[to],
            dst_ref=got_ref.at[me],
            send_sem=send_sem.at[flips],
            recv_sem=recv_sem.at[flips],
            device_id={"slab": to},
        )
        copy.start()
        copies.append(copy)
    own.wait()
    for copy in copies:
        copy.wait()


def exchange(blocks, identity, space):
    size = blocks.shape[0]
    return pl.pallas_call(
        functools.partial(exchange_kernel, size),
        out_shape=jax.ShapeDtypeStruct(blocks.shape, blocks.dtype),
        in_specs=[pl.BlockSpec(memory_space=space)],
        out_specs=pl.BlockSpec(memory_space=space),
        scratch_shapes=[
            pltpu.SemaphoreType.DMA((size,)),
            pltpu.SemaphoreType.DMA((size,)),
            pltpu.SemaphoreType.DMA,
        ],
        compiler_params=pltpu.CompilerParams(
            collective_id=identity, has_side_effects=True, vmem_limit_bytes=32 << 20
        ),
    )(blocks)


def halo_kernel(size, plane_ref, out_ref, send_sem, recv_sem):
    me = lax.axis_index("slab")
    sides = (lax.rem(me + 1, size), lax.rem(me + size - 1, size))
    barrier = pltpu.get_barrier_semaphore()
    for side in sides:
        pl.semaphore_signal(barrier, inc=1, device_id={"slab": side})
    pl.semaphore_wait(barrier, 2)
    copies = []
    for at, side in enumerate(sides):
        copy = pltpu.make_async_remote_copy(
            src_ref=plane_ref,
            dst_ref=out_ref.at[at],
            send_sem=send_sem.at[at],
            recv_sem=recv_sem.at[at],
            device_id={"slab": side},
        )
        copy.start()
        copies.append(copy)
    for copy in copies:
        copy.wait()


def halos(plane, identity):
    size = lax.axis_size("slab")
    me = lax.axis_index("slab")
    got = pl.pallas_call(
        functools.partial(halo_kernel, size),
        out_shape=jax.ShapeDtypeStruct((2,) + plane.shape, plane.dtype),
        in_specs=[pl.BlockSpec(memory_space=pltpu.VMEM)],
        out_specs=pl.BlockSpec(memory_space=pltpu.VMEM),
        scratch_shapes=[pltpu.SemaphoreType.DMA((2,)), pltpu.SemaphoreType.DMA((2,))],
        compiler_params=pltpu.CompilerParams(
            collective_id=identity, has_side_effects=True, vmem_limit_bytes=16 << 20
        ),
    )(plane)
    keep = jnp.stack([me > 0, me < size - 1]).astype(jnp.float32)
    return got, keep


def dft_parts(length):
    position = np.arange(length)
    angles = (position[:, None] * position[None, :] % length) * (2.0 * math.pi / length)
    scale = 1.0 / math.sqrt(length)
    cosine = (np.cos(angles) * scale).astype(jnp.bfloat16)
    sine = (np.sin(angles) * scale).astype(jnp.bfloat16)
    return cosine, sine


def table_wide(length):
    cosine, sine = dft_parts(length)
    gap = -length % 128
    return np.concatenate([cosine, np.zeros((length, gap), cosine.dtype), sine], axis=1)


def table_square(length):
    cosine, sine = dft_parts(length)
    upper = np.concatenate([cosine, sine], axis=1)
    lower = np.concatenate([-sine, cosine], axis=1)
    return np.concatenate([upper, lower], axis=0)


def dot(left, right):
    return jnp.dot(left, right, preferred_element_type=jnp.float32)


def gradient_kernel(
    maps_ref, measured_ref, gate_ref, image_ref, wide_ref, square_ref, turned_ref,
    noisy_ref, low_ref, total_ref,
):
    step = pl.program_id(0)
    planes, lines = gate_ref.shape
    start = wide_ref.shape[1] - lines
    f32, bf16 = jnp.float32, jnp.bfloat16

    @pl.when(step == 0)
    def _():
        total_ref[...] = jnp.zeros_like(total_ref)

    image_re = image_ref[0].astype(bf16).astype(f32)
    image_im = image_ref[1].astype(bf16).astype(f32)
    gate = gate_ref[...].astype(f32)
    gate = jnp.concatenate([gate, gate], axis=0)
    wide = wide_ref[...]
    for coil in range(maps_ref.shape[1]):
        maps_re = maps_ref[0, coil].astype(f32)
        maps_im = maps_ref[1, coil].astype(f32)
        both = jnp.concatenate(
            [maps_re * image_re - maps_im * image_im, maps_re * image_im + maps_im * image_re],
            axis=0,
        ).astype(bf16)
        out = dot(both, wide)
        cos_part, sin_part = out[:, :lines], out[:, start:]
        hybrid = jnp.concatenate(
            [cos_part[:planes] + sin_part[planes:], cos_part[planes:] - sin_part[:planes]], axis=0
        ).astype(bf16)
        predicted = dot(square_ref[...], hybrid)
        seen = jnp.concatenate([measured_ref[0, coil], measured_ref[1, coil]], axis=0)
        residual = (gate * (predicted - seen.astype(f32))).astype(bf16)
        back_z = dot(turned_ref[...], residual).astype(bf16)
        out = dot(back_z, wide)
        cos_part, sin_part = out[:, :lines], out[:, start:]
        back_re = cos_part[:planes] - sin_part[planes:]
        back_im = cos_part[planes:] + sin_part[:planes]
        total_ref[0] += maps_re * back_re + maps_im * back_im
        total_ref[1] += maps_re * back_im - maps_im * back_re

    @pl.when(step == pl.num_programs(0) - 1)
    def _():
        noisy = image_ref[...] - total_ref[...]
        noisy_ref[...] = noisy
        low_ref[...] = noisy.astype(bf16)


def gradient_step(maps, measured, gate, image, wide, square, turned):
    parts, coils, planes, lines = measured.shape
    group = 2
    whole = lambda shape: pl.BlockSpec(shape, lambda i: (0,) * len(shape))
    by_coil = pl.BlockSpec((parts, group, planes, lines), lambda i: (0, i, 0, 0))
    shape = (parts, planes, lines)
    return pl.pallas_call(
        gradient_kernel,
        grid=(coils // group,),
        in_specs=[by_coil, by_coil, whole(gate.shape), whole(shape)]
        + [whole(t.shape) for t in (wide, square, turned)],
        out_specs=[whole(shape), whole(shape)],
        out_shape=[
            jax.ShapeDtypeStruct(shape, jnp.float32),
            jax.ShapeDtypeStruct(shape, jnp.bfloat16),
        ],
        scratch_shapes=[pltpu.VMEM(shape, jnp.float32)],
        compiler_params=pltpu.CompilerParams(vmem_limit_bytes=40 << 20),
    )(maps, measured, gate, image, wide, square, turned)


GROUP = 8


def denoise_kernel(noisy_ref, low_ref, halo_ref, keep_ref, one_ref, two_ref, three_ref, out_ref, act_ref):
    parts, planes, lines = noisy_ref.shape
    hidden = two_ref.shape[0] // GROUP
    f32, bf16 = jnp.float32, jnp.bfloat16
    edge = jnp.zeros((planes, 1), f32)
    taps = []
    for read in range(3):
        for part in range(parts):
            if read == 1:
                plane = low_ref[part].astype(f32)
            else:
                side = read // 2
                plane = halo_ref[side, part].astype(f32) * keep_ref[side]
            taps.append(jnp.concatenate([edge, plane[:, :-1]], axis=1))
            taps.append(plane)
            taps.append(jnp.concatenate([plane[:, 1:], edge], axis=1))
    act_ref[:hidden] = jnp.zeros((hidden, lines), bf16)
    act_ref[(planes + 1) * hidden :] = jnp.zeros((hidden, lines), bf16)
    rows = GROUP * hidden
    for z in range(0, planes, GROUP):
        patch = jnp.concatenate([tap[z : z + GROUP] for tap in taps], axis=0).astype(bf16)
        first = dot(one_ref[...], patch)
        at = (z + 1) * hidden
        act_ref[at : at + rows] = jnp.maximum(first, 0.0).astype(bf16)
    for z in range(0, planes, GROUP):
        window = act_ref[z * hidden : (z + GROUP + 2) * hidden]
        second = jnp.maximum(dot(two_ref[...], window), 0.0).astype(bf16)
        last = dot(three_ref[...], second)
        for part in range(parts):
            add = last[part * GROUP : (part + 1) * GROUP]
            out_ref[part, z : z + GROUP] = noisy_ref[part, z : z + GROUP] + add


def denoise_weights(conv_plane, conv_depth, conv_output):
    hidden, parts = conv_plane.shape[:2]
    eye = np.eye(GROUP, dtype=np.float32).astype(jnp.bfloat16)
    taps = jnp.transpose(conv_plane, (0, 2, 1, 3)).reshape(hidden, -1)
    one = eye[:, None, None, :] * taps[None, :, :, None]
    one = one.reshape(GROUP * hidden, -1)
    shifts = np.stack([np.eye(GROUP, GROUP + 2, t, np.float32) for t in range(3)])
    shifts = shifts.astype(jnp.bfloat16)
    two = sum(shifts[t][:, None, :, None] * conv_depth[:, t, :][None, :, None, :] for t in range(3))
    two = two.reshape(GROUP * hidden, -1)
    three = eye[None, :, :, None] * conv_output[:, None, None, :]
    three = three.reshape(parts * GROUP, -1)
    return one, two, three


def denoise(noisy, low, weights, identity):
    got, keep = halos(low, identity)
    parts, planes, lines = noisy.shape
    hidden = weights[1].shape[0] // GROUP
    vmem = pl.BlockSpec(memory_space=pltpu.VMEM)
    return pl.pallas_call(
        denoise_kernel,
        out_shape=jax.ShapeDtypeStruct(noisy.shape, jnp.float32),
        in_specs=[vmem] * 3 + [pl.BlockSpec(memory_space=pltpu.SMEM)] + [vmem] * 3,
        out_specs=vmem,
        scratch_shapes=[pltpu.VMEM(((planes + 2) * hidden, lines), jnp.bfloat16)],
        compiler_params=pltpu.CompilerParams(vmem_limit_bytes=40 << 20),
    )(noisy, low, got, keep, *weights)


def body(measured, coil_maps, start_image, line_mask, conv_plane, conv_depth, conv_output):
    parts, coils, slices, reads, lines = coil_maps.shape
    size = lax.axis_size("slab")
    wide = jnp.asarray(table_wide(lines))
    square = table_square(slices * size)
    square, turned = jnp.asarray(square), jnp.asarray(square.T)
    weights = denoise_weights(conv_plane, conv_depth, conv_output)
    sent = jnp.concatenate([coil_maps, start_image.astype(jnp.bfloat16)[:, None]], axis=1)
    sent = jnp.moveaxis(sent, 3, 0).reshape(size, -1, lines)
    got = exchange(sent, 1, pl.ANY).reshape(size, parts, coils + 1, slices, lines)
    maps = jnp.moveaxis(got, 0, 2).reshape(parts, coils + 1, size * slices, lines)
    estimate = maps[:, coils].astype(jnp.float32)
    seen = measured.reshape(parts, coils, size * slices, lines)
    for index_pass in range(PASSES):
        noisy, low = gradient_step(maps, seen, line_mask, estimate, wide, square, turned)
        estimate = denoise(noisy, low, weights, 3 + index_pass)
    leave = estimate.astype(jnp.bfloat16).reshape(parts, size, slices, lines)
    leave = jnp.moveaxis(leave, 1, 0).reshape(size, parts * slices, lines)
    out = exchange(leave, 2, pltpu.VMEM).reshape(reads, parts, slices, lines)
    return jnp.transpose(out, (1, 2, 0, 3)).astype(jnp.float32)


def solution(mesh):
    in_specs = (
        P("exam", None, None, "slab", None),
        P("exam", None, "slab", None, None),
        P("exam", "slab", None, None),
        P("exam", None),
        P(),
        P(),
        P(),
    )
    out_specs = P("exam", "slab", None, None)
    return jax.shard_map(body, mesh=mesh, in_specs=in_specs, out_specs=out_specs, check_vma=False)
```

time: 178 us -> 176 us (0.989)
  Pallas kernels: 102 us -> 148 us
  matrix products: 40.4 us -> 0 us
  other arithmetic: 16.5 us -> 7.42 us
  local copies, waits for them, and re-layouts: 17.9 us -> 19.8 us
    pallas_call x0 -> x4, Pallas kernels: none -> 46.4 us  [the longest x2 35 us: gradient_step(): pl.pallas_call(gradient_kernel, grid=(coils // group,), in_specs=[by_coil...]
    dot_general x8 -> x0, matrix products: 36.8 us -> none  [the longest x2 11.6 us: residual_back(): jnp.einsum('qkpn,qckxy->pcnxy', table_z, residual, preferred_element_type...]
    unnamed x31 -> x26, local copies, waits for them, and re-layouts: 1.48 us -> 13 us
    another operation x13 -> x0, other arithmetic: 9.11 us -> none
    slice x2 -> x0, local copies, waits for them, and re-layouts: 7.39 us -> none  [denoise(): padded[:, t:t + planes]]
    another operation x2 -> x0, local copies, waits for them, and re-layouts: 3.73 us -> none  [denoise(): jnp.stack([before, flat, after], axis=2).reshape(parts, planes, 3, lines)]
    conv_general_dilated x2 -> x0, matrix products: 3.62 us -> none  [denoise(): lax.conv_general_dilated(wide, conv_plane, (1, 1), ((0, 0), (1, 1)), dime...]
    dot_general x2 -> x0, local copies, waits for them, and re-layouts: 3.02 us -> none  [denoise(): jnp.einsum('pi,izxy->pzxy', conv_output, act_two, preferred_element_type=...]
where the time goes in v3:
time: 176 us
  Pallas kernels  148 us (84%)
  local copies, waits for them, and re-layouts  19.8 us (11%)
  other arithmetic  7.42 us (4%)
    pallas_call x2, Pallas kernels, exchange(): pl.pallas_call(functools.partial(exchange_kernel, size), out_shape=jax.Sh...  79.9 us
    pallas_call x2, Pallas kernels, gradient_step(): pl.pallas_call(gradient_kernel, grid=(coils // group,), in_specs=[by_coil...  35 us
    pallas_call x2, Pallas kernels, halos(): pl.pallas_call(functools.partial(halo_kernel, size), out_shape=jax.ShapeD...  22.1 us
    unnamed x26, local copies, waits for them, and re-layouts  13 us
    pallas_call x2, Pallas kernels, denoise(): pl.pallas_call(denoise_kernel, out_shape=jax.ShapeDtypeStruct(noisy.shape...  11.4 us

profile of v3, /device:TPU:0, one launch (start us, length us, event | category | flops | bytes accessed | tf_op | source)
XLA Modules:
  0.0 175.8 jit_solution(14364870101694309495)
XLA Ops:
  0.0 0.0 copy-start.11
  0.0 0.1 add_convert_fusion.keep_ref
  0.1 0.8 copy.29
  0.9 0.8 slice_bitcast_fusion.3
  1.7 0.1 copy.30
  1.8 0.1 copy.32
  1.9 0.1 copy.31
  1.9 0.8 broadcast_multiply_fusion.1
  2.7 0.1 mul.122.three_ref
  2.8 1.7 copy.36.gate_ref
  4.6 1.7 convert_bitcast_fusion.1
  6.3 0.8 broadcast_multiply_fusion
  7.0 0.2 mul.102
  7.2 0.8 copy.34.one_ref
  8.0 1.8 multiply_add_fusion
  9.8 1.6 add.14
  11.3 0.2 copy.35.two_ref
  11.5 0.0 copy-done.11
  11.5 1.5 maximum_bitcast_fusion
  13.0 0.7 copy.25
  13.8 61.6 %shard_map.145 = bf16[16,272,320]{2,1,0:T(8,128)(2,1)S(1)} custom-call(bf16[16,272,320]{2,1,0:T(8,128)(2,1)S(1)} %bitcast.58), custom_call_target="tpu_custom_call" | custom-call | tf_op jit(solution)/shard_map/pallas_call | solution.py:63
  75.4 0.6 copy.44
  75.9 0.8 fusion.image_ref
  76.7 4.6 %copy.27 = bf16[2,16,128,1,320]{4,2,1,0,3:T(8,128)(2,1)} copy(bf16[2,16,128,1,320]{2,4,3,1,0:T(8,128)(2,1)} %param.15) | data formatting | bytes 5242880 | tf_op args[0]
  81.3 0.0 copy-start
  81.3 1.9 %copy-done = bf16[2,16,128,1,320]{4,2,1,0,3:T(8,128)(2,1)S(1)} copy-done((bf16[2,16,128,1,320]{4,2,1,0,3:T(8,128)(2,1)S(1)}, bf16[2,16,128,1,320]{4,2,1,0,3:T(8,128)(2,1)}, u32[]{:S(2)}) %copy-start) | copy-done | bytes 2621464
  83.2 0.0 copy-start.2
  83.2 1.0 copy-done.2
  84.2 0.0 copy-start.4
  84.2 0.9 copy-done.4
  85.1 0.0 copy-start.5
  85.1 1.0 copy-done.5
  86.1 0.9 copy-done.7
  87.0 0.9 copy-done.9
  88.0 0.0 copy-start.10
  88.0 17.4 %shard_map.146 = (f32[2,128,320]{2,1,0:T(8,128)S(1)}, bf16[2,128,320]{2,1,0:T(8,128)(2,1)S(1)}) custom-call(bf16[2,17,128,320]{3,2,1,0:T(8,128)(2,1)S(1)} %bitcast.54, bf16[2,16,128,320]{3,2,1,0:T(8,128)(2,1)S(1)} %bitcast.56, s32[128,320]{1,0:T(8,128)S(1)} %copy-done.4, f32[2,128,320]{2,1,0:T(8,128)S(1)} %copy-done.5, bf16[320,704]{1,0:T(8,128)(2,1)S(1)} %copy-done.2, ...), custom_call_target="tpu_custom_call" | custom-call | tf_op jit(solution)/shard_map/pallas_call | solution.py:198
  105.4 7.9 %shard_map.147.halo_ref = bf16[2,2,128,320]{3,2,1,0:T(8,128)(2,1)S(1)} custom-call(bf16[2,128,320]{2,1,0:T(8,128)(2,1)S(1)} %get-tuple-element.10.plane_ref.low_ref), custom_call_target="tpu_custom_call" | custom-call | tf_op jit(solution)/shard_map/pallas_call | solution.py:104
  113.3 0.0 copy-done.6
  113.3 5.7 %shard_map.148.image_ref = f32[2,128,320]{2,1,0:T(8,128)S(1)} custom-call(f32[2,128,320]{2,1,0:T(8,128)S(1)} %get-tuple-element.9.noisy_ref, bf16[2,128,320]{2,1,0:T(8,128)(2,1)S(1)} %get-tuple-element.10.plane_ref.low_ref, bf16[2,2,128,320]{3,2,1,0:T(8,128)(2,1)S(1)} %shard_map.147.halo_ref, f32[2]{0:T(128)S(1)} %add_convert_fusion.keep_ref, ...), custom_call_target="tpu_custom_call" | custom-call | tf_op jit(solution)/shard_map/pallas_call | solution.py:269
  119.0 0.0 copy-done.1
  119.0 0.0 copy-done.3
  119.0 0.0 copy-done.8
  119.0 0.0 copy-done.10
  119.0 17.6 %shard_map.149 = (f32[2,128,320]{2,1,0:T(8,128)S(1)}, bf16[2,128,320]{2,1,0:T(8,128)(2,1)S(1)}) custom-call(bf16[2,17,128,320]{3,2,1,0:T(8,128)(2,1)S(1)} %bitcast.55, bf16[2,16,128,320]{3,2,1,0:T(8,128)(2,1)S(1)} %bitcast.57, s32[128,320]{1,0:T(8,128)S(1)} %copy-done.4, f32[2,128,320]{2,1,0:T(8,128)S(1)} %shard_map.148.image_ref, ...), custom_call_target="tpu_custom_call" | custom-call | tf_op jit(solution)/shard_map/pallas_call | solution.py:198
  136.6 14.3 %shard_map.150.halo_ref = bf16[2,2,128,320]{3,2,1,0:T(8,128)(2,1)S(1)} custom-call(bf16[2,128,320]{2,1,0:T(8,128)(2,1)S(1)} %get-tuple-element.12.plane_ref.low_ref), custom_call_target="tpu_custom_call" | custom-call | tf_op jit(solution)/shard_map/pallas_call | solution.py:104
  150.9 5.7 %shard_map.151 = f32[2,128,320]{2,1,0:T(8,128)S(1)} custom-call(f32[2,128,320]{2,1,0:T(8,128)S(1)} %get-tuple-element.11.noisy_ref, bf16[2,128,320]{2,1,0:T(8,128)(2,1)S(1)} %get-tuple-element.12.plane_ref.low_ref, bf16[2,2,128,320]{3,2,1,0:T(8,128)(2,1)S(1)} %shard_map.150.halo_ref, f32[2]{0:T(128)S(1)} %add_convert_fusion.keep_ref, ...), custom_call_target="tpu_custom_call" | custom-call | tf_op jit(solution)/shard_map/pallas_call | solution.py:269
  156.6 18.3 %shard_map.152 = bf16[16,16,320]{2,1,0:T(8,128)(2,1)S(1)} custom-call(bf16[16,16,320]{2,1,0:T(8,128)(2,1)S(1)} %copy_bitcast_fusion.2.sent_ref), custom_call_target="tpu_custom_call" | custom-call | tf_op jit(solution)/shard_map/pallas_call | solution.py:63
  174.9 0.9 copy.45
  (9 shorter events, 0.1 us)
Async XLA Ops:
  0.0 11.5 %copy-start.11 = (bf16[2,16,8,16,320]{4,3,2,1,0:T(8,128)(2,1)S(1)}, bf16[2,16,8,16,320]{4,3,2,1,0:T(8,128)(2,1)}, u32[]{:S(2)}) copy-start(bf16[2,16,8,16,320]{4,3,2,1,0:T(8,128)(2,1)} %param.16) | copy-start | bytes 7864324
  81.3 1.9 %copy-start = (bf16[2,16,128,1,320]{4,2,1,0,3:T(8,128)(2,1)S(1)}, bf16[2,16,128,1,320]{4,2,1,0,3:T(8,128)(2,1)}, u32[]{:S(2)}) copy-start(bf16[2,16,128,1,320]{4,2,1,0,3:T(8,128)(2,1)} %copy.27) | copy-start | bytes 7864324
  83.2 1.0 copy-start.2
  84.2 0.9 copy-start.4
  85.1 1.0 copy-start.5
  86.1 0.9 copy-start.7
  87.0 0.9 copy-start.9
  87.9 25.3 %copy-start.6 = (bf16[256,144]{1,0:T(8,128)(2,1)S(1)}, bf16[256,144]{1,0:T(8,128)(2,1)}, u32[]{:S(2)}) copy-start(bf16[256,144]{1,0:T(8,128)(2,1)} %copy.34.one_ref) | copy-start | bytes 221188
  87.9 31.0 %copy-start.1 = (bf16[2,16,128,1,320]{4,2,1,0,3:T(8,128)(2,1)S(1)}, bf16[2,16,128,1,320]{4,2,1,0,3:T(8,128)(2,1)}, u32[]{:S(2)}) copy-start(bf16[2,16,128,1,320]{4,2,1,0,3:T(8,128)(2,1)} %copy.27) | copy-start | bytes 7864324
  87.9 31.0 %copy-start.3 = (bf16[320,704]{1,0:T(8,128)(2,1)S(1)}, bf16[320,704]{1,0:T(8,128)(2,1)}, u32[]{:S(2)}) copy-start(bf16[320,704]{1,0:T(8,128)(2,1)} %constant.24.clone.wide_ref) | copy-start | bytes 1351684
  88.0 31.0 %copy-start.8 = (bf16[256,256]{1,0:T(8,128)(2,1)S(1)}, bf16[256,256]{1,0:T(8,128)(2,1)}, u32[]{:S(2)}) copy-start(bf16[256,256]{1,0:T(8,128)(2,1)} %constant.26.clone.turned_ref) | copy-start | bytes 393220
  88.0 31.0 %copy-start.10 = (bf16[256,256]{1,0:T(8,128)(2,1)S(1)}, bf16[256,256]{1,0:T(8,128)(2,1)}, u32[]{:S(2)}) copy-start(bf16[256,256]{1,0:T(8,128)(2,1)} %constant.25.clone.square_ref) | copy-start | bytes 393220

commit v4 on v3

--- a/solution.py
+++ b/solution.py
@@ -78,30 +78,53 @@
 
 def halo_kernel(size, plane_ref, out_ref, send_sem, recv_sem):
     me = lax.axis_index("slab")
-    sides = (lax.rem(me + 1, size), lax.rem(me + size - 1, size))
     barrier = pltpu.get_barrier_semaphore()
-    for side in sides:
-        pl.semaphore_signal(barrier, inc=1, device_id={"slab": side})
-    pl.semaphore_wait(barrier, 2)
     copies = []
-    for at, side in enumerate(sides):
-        copy = pltpu.make_async_remote_copy(
-            src_ref=plane_ref,
-            dst_ref=out_ref.at[at],
-            send_sem=send_sem.at[at],
-            recv_sem=recv_sem.at[at],
-            device_id={"slab": side},
+    for at, step in enumerate((1, -1)):
+        side = lax.rem(me + step + size, size)
+        copies.append(
+            pltpu.make_async_remote_copy(
+                src_ref=plane_ref,
+                dst_ref=out_ref.at[at],
+                send_sem=send_sem.at[at],
+                recv_sem=recv_sem.at[at],
+                device_id={"slab": side},
+            )
         )
-        copy.start()
-        copies.append(copy)
-    for copy in copies:
-        copy.wait()
+    has = (me < size - 1, me > 0)
+    for at, step in enumerate((1, -1)):
+
+        @pl.when(has[at])
+        def _():
+            side = lax.rem(me + step + size, size)
+            pl.semaphore_signal(barrier, inc=1, device_id={"slab": side})
+
+    pl.semaphore_wait(barrier, has[0].astype(jnp.int32) + has[1].astype(jnp.int32))
+
+    for at in range(2):
+
+        @pl.when(has[at])
+        def _():
+            copies[at].start()
+
+    for at in range(2):
+
+        @pl.when(jnp.logical_not(has[1 - at]))
+        def _():
+            out_ref[at] = jnp.zeros(out_ref.shape[1:], out_ref.dtype)
+
+        @pl.when(has[1 - at])
+        def _():
+            copies[at].wait_recv()
+
+        @pl.when(has[at])
+        def _():
+            copies[at].wait_send()
 
 
 def halos(plane, identity):
     size = lax.axis_size("slab")
-    me = lax.axis_index("slab")
-    got = pl.pallas_call(
+    return pl.pallas_call(
         functools.partial(halo_kernel, size),
         out_shape=jax.ShapeDtypeStruct((2,) + plane.shape, plane.dtype),
         in_specs=[pl.BlockSpec(memory_space=pltpu.VMEM)],
@@ -111,8 +134,6 @@
             collective_id=identity, has_side_effects=True, vmem_limit_bytes=16 << 20
         ),
     )(plane)
-    keep = jnp.stack([me > 0, me < size - 1]).astype(jnp.float32)
-    return got, keep
 
 
 def dft_parts(length):
@@ -159,14 +180,18 @@
     gate = gate_ref[...].astype(f32)
     gate = jnp.concatenate([gate, gate], axis=0)
     wide = wide_ref[...]
-    for coil in range(maps_ref.shape[1]):
+    coils = maps_ref.shape[1]
+    rows = 2 * planes
+    both = []
+    for coil in range(coils):
         maps_re = maps_ref[0, coil].astype(f32)
         maps_im = maps_ref[1, coil].astype(f32)
-        both = jnp.concatenate(
-            [maps_re * image_re - maps_im * image_im, maps_re * image_im + maps_im * image_re],
-            axis=0,
-        ).astype(bf16)
-        out = dot(both, wide)
+        both.append((maps_re * image_re - maps_im * image_im).astype(bf16))
+        both.append((maps_re * image_im + maps_im * image_re).astype(bf16))
+    forward = dot(jnp.concatenate(both, axis=0), wide)
+    back = []
+    for coil in range(coils):
+        out = forward[coil * rows : (coil + 1) * rows]
         cos_part, sin_part = out[:, :lines], out[:, start:]
         hybrid = jnp.concatenate(
             [cos_part[:planes] + sin_part[planes:], cos_part[planes:] - sin_part[:planes]], axis=0
@@ -174,13 +199,21 @@
         predicted = dot(square_ref[...], hybrid)
         seen = jnp.concatenate([measured_ref[0, coil], measured_ref[1, coil]], axis=0)
         residual = (gate * (predicted - seen.astype(f32))).astype(bf16)
-        back_z = dot(turned_ref[...], residual).astype(bf16)
-        out = dot(back_z, wide)
+        back.append(dot(turned_ref[...], residual).astype(bf16))
+    inverse = dot(jnp.concatenate(back, axis=0), wide)
+    sum_re = total_ref[0]
+    sum_im = total_ref[1]
+    for coil in range(coils):
+        maps_re = maps_ref[0, coil].astype(f32)
+        maps_im = maps_ref[1, coil].astype(f32)
+        out = inverse[coil * rows : (coil + 1) * rows]
         cos_part, sin_part = out[:, :lines], out[:, start:]
         back_re = cos_part[:planes] - sin_part[planes:]
         back_im = cos_part[planes:] + sin_part[:planes]
-        total_ref[0] += maps_re * back_re + maps_im * back_im
-        total_ref[1] += maps_re * back_im - maps_im * back_re
+        sum_re += maps_re * back_re + maps_im * back_im
+        sum_im += maps_re * back_im - maps_im * back_re
+    total_ref[0] = sum_re
+    total_ref[1] = sum_im
 
     @pl.when(step == pl.num_programs(0) - 1)
     def _():
@@ -191,7 +224,7 @@
 
 def gradient_step(maps, measured, gate, image, wide, square, turned):
     parts, coils, planes, lines = measured.shape
-    group = 2
+    group = math.gcd(coils, 4)
     whole = lambda shape: pl.BlockSpec(shape, lambda i: (0,) * len(shape))
     by_coil = pl.BlockSpec((parts, group, planes, lines), lambda i: (0, i, 0, 0))
     shape = (parts, planes, lines)
@@ -206,26 +239,68 @@
             jax.ShapeDtypeStruct(shape, jnp.bfloat16),
         ],
         scratch_shapes=[pltpu.VMEM(shape, jnp.float32)],
-        compiler_params=pltpu.CompilerParams(vmem_limit_bytes=40 << 20),
+        compiler_params=pltpu.CompilerParams(vmem_limit_bytes=58 << 20),
     )(maps, measured, gate, image, wide, square, turned)
 
 
 GROUP = 8
 
 
-def denoise_kernel(noisy_ref, low_ref, halo_ref, keep_ref, one_ref, two_ref, three_ref, out_ref, act_ref):
+def spots(shape):
+    return lax.broadcasted_iota(jnp.int32, shape, 0), lax.broadcasted_iota(jnp.int32, shape, 1)
+
+
+def chosen(condition):
+    return jnp.where(condition, 1.0, 0.0).astype(jnp.bfloat16)
+
+
+def plane_weights(plane):
+    hidden, taps = plane.shape
+    bits, group_bits = hidden.bit_length() - 1, GROUP.bit_length() - 1
+    row, col = spots((taps, taps * GROUP))
+    spread = dot(jnp.concatenate([plane] * GROUP, axis=0), chosen(row == (col >> group_bits)))
+    row, col = spots(spread.shape)
+    return jnp.where((row >> bits) == (col & (GROUP - 1)), spread, 0.0).astype(jnp.bfloat16)
+
+
+def depth_weights(depth):
+    hidden, taps = depth.shape
+    bits = hidden.bit_length() - 1
+    tall = jnp.concatenate([depth] * GROUP, axis=0)
+    total = jnp.zeros((GROUP * hidden, (GROUP + 2) * hidden), jnp.float32)
+    for t in range(3):
+        row, col = spots((taps, total.shape[1]))
+        spread = dot(tall, chosen(row == (col & (hidden - 1)) + t * hidden))
+        row, col = spots(total.shape)
+        total = jnp.where((col >> bits) - (row >> bits) == t, spread, total)
+    return total.astype(jnp.bfloat16)
+
+
+def output_weights(output):
+    parts, hidden = output.shape
+    bits = hidden.bit_length() - 1
+    wide = output.astype(jnp.float32)
+    tall = jnp.concatenate(
+        [jnp.broadcast_to(wide[p : p + 1], (GROUP, hidden)) for p in range(parts)], axis=0
+    ).astype(jnp.bfloat16)
+    row, col = spots((hidden, GROUP * hidden))
+    spread = dot(tall, chosen(row == (col & (hidden - 1))))
+    row, col = spots(spread.shape)
+    return jnp.where((row & (GROUP - 1)) == (col >> bits), spread, 0.0).astype(jnp.bfloat16)
+
+
+def denoise_kernel(noisy_ref, low_ref, halo_ref, plane_ref, depth_ref, output_ref, out_ref, act_ref):
     parts, planes, lines = noisy_ref.shape
-    hidden = two_ref.shape[0] // GROUP
+    hidden = depth_ref.shape[0]
     f32, bf16 = jnp.float32, jnp.bfloat16
+    one = plane_weights(plane_ref[...])
+    two = depth_weights(depth_ref[...])
+    three = output_weights(output_ref[...])
     edge = jnp.zeros((planes, 1), f32)
     taps = []
-    for read in range(3):
-        for part in range(parts):
-            if read == 1:
-                plane = low_ref[part].astype(f32)
-            else:
-                side = read // 2
-                plane = halo_ref[side, part].astype(f32) * keep_ref[side]
+    for part in range(parts):
+        for plane in (halo_ref[0, part], low_ref[part], halo_ref[1, part]):
+            plane = plane.astype(f32)
             taps.append(jnp.concatenate([edge, plane[:, :-1]], axis=1))
             taps.append(plane)
             taps.append(jnp.concatenate([plane[:, 1:], edge], axis=1))
@@ -234,46 +309,31 @@
     rows = GROUP * hidden
     for z in range(0, planes, GROUP):
         patch = jnp.concatenate([tap[z : z + GROUP] for tap in taps], axis=0).astype(bf16)
-        first = dot(one_ref[...], patch)
+        first = dot(one, patch)
         at = (z + 1) * hidden
         act_ref[at : at + rows] = jnp.maximum(first, 0.0).astype(bf16)
     for z in range(0, planes, GROUP):
         window = act_ref[z * hidden : (z + GROUP + 2) * hidden]
-        second = jnp.maximum(dot(two_ref[...], window), 0.0).astype(bf16)
-        last = dot(three_ref[...], second)
+        second = jnp.maximum(dot(two, window), 0.0).astype(bf16)
+        last = dot(three, second)
         for part in range(parts):
             add = last[part * GROUP : (part + 1) * GROUP]
             out_ref[part, z : z + GROUP] = noisy_ref[part, z : z + GROUP] + add
 
 
-def denoise_weights(conv_plane, conv_depth, conv_output):
-    hidden, parts = conv_plane.shape[:2]
-    eye = np.eye(GROUP, dtype=np.float32).astype(jnp.bfloat16)
-    taps = jnp.transpose(conv_plane, (0, 2, 1, 3)).reshape(hidden, -1)
-    one = eye[:, None, None, :] * taps[None, :, :, None]
-    one = one.reshape(GROUP * hidden, -1)
-    shifts = np.stack([np.eye(GROUP, GROUP + 2, t, np.float32) for t in range(3)])
-    shifts = shifts.astype(jnp.bfloat16)
-    two = sum(shifts[t][:, None, :, None] * conv_depth[:, t, :][None, :, None, :] for t in range(3))
-    two = two.reshape(GROUP * hidden, -1)
-    three = eye[None, :, :, None] * conv_output[:, None, None, :]
-    three = three.reshape(parts * GROUP, -1)
-    return one, two, three
-
-
 def denoise(noisy, low, weights, identity):
-    got, keep = halos(low, identity)
+    got = halos(low, identity)
     parts, planes, lines = noisy.shape
-    hidden = weights[1].shape[0] // GROUP
+    hidden = weights[1].shape[0]
     vmem = pl.BlockSpec(memory_space=pltpu.VMEM)
     return pl.pallas_call(
         denoise_kernel,
         out_shape=jax.ShapeDtypeStruct(noisy.shape, jnp.float32),
-        in_specs=[vmem] * 3 + [pl.BlockSpec(memory_space=pltpu.SMEM)] + [vmem] * 3,
+        in_specs=[vmem] * 6,
         out_specs=vmem,
         scratch_shapes=[pltpu.VMEM(((planes + 2) * hidden, lines), jnp.bfloat16)],
         compiler_params=pltpu.CompilerParams(vmem_limit_bytes=40 << 20),
-    )(noisy, low, got, keep, *weights)
+    )(noisy, low, got, *weights)
 
 
 def body(measured, coil_maps, start_image, line_mask, conv_plane, conv_depth, conv_output):
@@ -282,7 +342,8 @@
     wide = jnp.asarray(table_wide(lines))
     square = table_square(slices * size)
     square, turned = jnp.asarray(square), jnp.asarray(square.T)
-    weights = denoise_weights(conv_plane, conv_depth, conv_output)
+    hidden = conv_plane.shape[0]
+    weights = (conv_plane.reshape(hidden, -1), conv_depth.reshape(hidden, -1), conv_output)
     sent = jnp.concatenate([coil_maps, start_image.astype(jnp.bfloat16)[:, None]], axis=1)
     sent = jnp.moveaxis(sent, 3, 0).reshape(size, -1, lines)
     got = exchange(sent, 1, pl.ANY).reshape(size, parts, coils + 1, slices, lines)

time: 176 us -> 164 us (0.932)
  Pallas kernels: 148 us -> 142 us
  other arithmetic: 7.42 us -> 4.36 us
  local copies, waits for them, and re-layouts: 19.8 us -> 17 us
    pallas_call x2, Pallas kernels: 35 us -> 29.5 us  [gradient_step(): pl.pallas_call(gradient_kernel, grid=(coils // group,), in_specs=[by_coil...]
    mul x8 -> x0, local copies, waits for them, and re-layouts: 2.08 us -> none  [the longest x4 1 us: denoise_weights(): shifts[t][:, None, :, None] * conv_depth[:, t, :][None, :, None, :]]
    unnamed x26 -> x22, local copies, waits for them, and re-layouts: 13 us -> 14.6 us
where the time goes in v4:
time: 164 us
  Pallas kernels  142 us (87%)
  local copies, waits for them, and re-layouts  17 us (10%)
  other arithmetic  4.36 us (3%)
    pallas_call x2, Pallas kernels, exchange(): pl.pallas_call(functools.partial(exchange_kernel, size), out_shape=jax.Sh...  79.9 us
    pallas_call x2, Pallas kernels, gradient_step(): pl.pallas_call(gradient_kernel, grid=(coils // group,), in_specs=[by_coil...  29.5 us
    pallas_call x2, Pallas kernels, halos(): pl.pallas_call(functools.partial(halo_kernel, size), out_shape=jax.ShapeD...  22.1 us
    unnamed x22, local copies, waits for them, and re-layouts  14.6 us
    pallas_call x2, Pallas kernels, denoise(): pl.pallas_call(denoise_kernel, out_shape=jax.ShapeDtypeStruct(noisy.shape...  10.6 us

profile of v4, /device:TPU:0, one launch (start us, length us, event | category | flops | bytes accessed | tf_op | source)
XLA Modules:
  0.0 163.6 jit_solution(8295465360459561551)
XLA Ops:
  0.0 0.7 copy.26
  0.7 0.1 copy.28.plane_ref
  0.8 0.8 copy.27
  1.6 0.1 reshape.34.depth_ref
  1.7 1.7 %copy.29.gate_ref = s32[128,320]{1,0:T(8,128)} copy(s32[128,320]{0,1:T(8,128)} %param.13) | data formatting | bytes 327680 | tf_op args[3]
  3.4 1.0 convert_bitcast_fusion.1
  4.4 2.5 %maximum_bitcast_fusion = bf16[16,2,17,8,320]{4,0,3,2,1:T(8,128)(2,1)S(1)} fusion(bf16[2,1,8,16,320]{4,3,2,1,0:T(8,128)(2,1)S(1)} %convert_bitcast_fusion.1, bf16[2,16,8,16,320]{4,3,2,1,0:T(8,128)(2,1)} %param.11), kind=kLoop, calls=%fused_computation | loop fusion | flops 1392640 | bytes 5570560 | tf_op jit(solution)/shard_map/transpose | solution.py:348
  6.9 0.7 copy.22
  7.6 61.6 %shard_map.100 = bf16[16,272,320]{2,1,0:T(8,128)(2,1)S(1)} custom-call(bf16[16,272,320]{2,1,0:T(8,128)(2,1)S(1)} %bitcast.34), custom_call_target="tpu_custom_call" | custom-call | tf_op jit(solution)/shard_map/pallas_call | solution.py:63
  69.2 0.6 copy.36
  69.8 0.0 copy-start.8
  69.8 0.8 fusion.image_ref
  70.6 5.0 %copy.24 = bf16[2,16,128,1,320]{4,2,1,0,3:T(8,128)(2,1)} copy(bf16[2,16,128,1,320]{2,4,3,1,0:T(8,128)(2,1)} %param.10) | data formatting | bytes 5242880 | tf_op args[0]
  75.7 0.0 copy-done.8
  75.7 0.0 copy-start.7
  75.7 14.8 %shard_map.101 = (f32[2,128,320]{2,1,0:T(8,128)}, bf16[2,128,320]{2,1,0:T(8,128)(2,1)}) custom-call(bf16[2,17,128,320]{3,2,1,0:T(8,128)(2,1)} %bitcast.37, bf16[2,16,128,320]{3,2,1,0:T(8,128)(2,1)} %bitcast.39, s32[128,320]{1,0:T(8,128)} %copy.29.gate_ref, f32[2,128,320]{2,1,0:T(8,128)} %fusion.image_ref, bf16[320,704]{1,0:T(8,128)(2,1)} %constant.6.clone.wide_ref, ...), custom_call_target="tpu_custom_call" | custom-call | tf_op jit(solution)/shard_map/pallas_call | solution.py:231
  90.5 0.0 copy-start.3
  90.5 0.9 copy-done.3
  91.4 2.6 %shard_map.102.halo_ref = bf16[2,2,128,320]{3,2,1,0:T(8,128)(2,1)S(1)} custom-call(bf16[2,128,320]{2,1,0:T(8,128)(2,1)S(1)} %copy-done.3), custom_call_target="tpu_custom_call" | custom-call | tf_op jit(solution)/shard_map/pallas_call | solution.py:127
  94.0 0.0 copy-done.7
  94.0 0.0 copy-start.4
  94.0 0.9 copy-done.4
  94.9 0.0 copy-start.6
  94.9 1.0 copy-done.6
  95.9 5.3 %shard_map.103.image_ref = f32[2,128,320]{2,1,0:T(8,128)S(1)} custom-call(f32[2,128,320]{2,1,0:T(8,128)S(1)} %copy-done.6, bf16[2,128,320]{2,1,0:T(8,128)(2,1)S(1)} %copy-done.4, bf16[2,2,128,320]{3,2,1,0:T(8,128)(2,1)S(1)} %shard_map.102.halo_ref, bf16[32,18]{1,0:T(8,128)(2,1)S(1)} %copy.28.plane_ref, bf16[32,96]{1,0:T(8,128)(2,1)S(1)} %reshape.34.depth_ref, ...), custom_call_target="tpu_custom_call" | custom-call | tf_op jit(solution)/shard_map/pallas_call | solution.py:329
  101.2 0.0 copy-start
  101.2 0.8 copy-done
  102.0 14.8 %shard_map.104 = (f32[2,128,320]{2,1,0:T(8,128)}, bf16[2,128,320]{2,1,0:T(8,128)(2,1)}) custom-call(bf16[2,17,128,320]{3,2,1,0:T(8,128)(2,1)} %bitcast.38, bf16[2,16,128,320]{3,2,1,0:T(8,128)(2,1)} %bitcast.40, s32[128,320]{1,0:T(8,128)} %copy.29.gate_ref, f32[2,128,320]{2,1,0:T(8,128)} %copy-done, bf16[320,704]{1,0:T(8,128)(2,1)} %constant.6.clone.wide_ref, ...), custom_call_target="tpu_custom_call" | custom-call | tf_op jit(solution)/shard_map/pallas_call | solution.py:231
  116.7 0.0 copy-start.1
  116.7 0.9 copy-done.1
  117.6 19.5 %shard_map.105.halo_ref = bf16[2,2,128,320]{3,2,1,0:T(8,128)(2,1)S(1)} custom-call(bf16[2,128,320]{2,1,0:T(8,128)(2,1)S(1)} %copy-done.1), custom_call_target="tpu_custom_call" | custom-call | tf_op jit(solution)/shard_map/pallas_call | solution.py:127
  137.1 0.0 copy-start.2
  137.1 0.9 copy-done.2
  138.1 0.0 copy-start.5
  138.1 1.0 copy-done.5
  139.0 5.3 %shard_map.106 = f32[2,128,320]{2,1,0:T(8,128)S(1)} custom-call(f32[2,128,320]{2,1,0:T(8,128)S(1)} %copy-done.5, bf16[2,128,320]{2,1,0:T(8,128)(2,1)S(1)} %copy-done.2, bf16[2,2,128,320]{3,2,1,0:T(8,128)(2,1)S(1)} %shard_map.105.halo_ref, bf16[32,18]{1,0:T(8,128)(2,1)S(1)} %copy.28.plane_ref, bf16[32,96]{1,0:T(8,128)(2,1)S(1)} %reshape.34.depth_ref, ...), custom_call_target="tpu_custom_call" | custom-call | tf_op jit(solution)/shard_map/pallas_call | solution.py:329
  144.4 18.3 %shard_map.107 = bf16[16,16,320]{2,1,0:T(8,128)(2,1)S(1)} custom-call(bf16[16,16,320]{2,1,0:T(8,128)(2,1)S(1)} %copy_bitcast_fusion.2.sent_ref), custom_call_target="tpu_custom_call" | custom-call | tf_op jit(solution)/shard_map/pallas_call | solution.py:63
  162.7 0.9 copy.37
  (3 shorter events, 0.1 us)
Async XLA Ops:
  69.8 5.9 %copy-start.8 = (bf16[16,2,17,8,320]{4,3,0,2,1:T(8,128)(2,1)}, bf16[16,2,17,8,320]{4,3,0,2,1:T(8,128)(2,1)S(1)}, u32[]{:S(2)}) copy-start(bf16[16,2,17,8,320]{4,3,0,2,1:T(8,128)(2,1)S(1)} %copy.36) | copy-start | bytes 8355844
  75.7 18.3 %copy-start.7 = (bf16[2,32]{1,0:T(2,128)(2,1)S(1)}, bf16[2,32]{1,0:T(2,128)(2,1)}, u32[]{:S(2)}) copy-start(bf16[2,32]{1,0:T(2,128)(2,1)} %output_ref.3) | copy-start | bytes 388
  90.5 0.9 copy-start.3
  94.0 0.9 copy-start.4
  94.9 1.0 copy-start.6
  101.2 0.8 copy-start
  116.7 0.9 copy-start.1
  137.1 0.9 copy-start.2
  138.1 1.0 copy-start.5

commit v5 on v4

--- a/solution.py
+++ b/solution.py
@@ -224,7 +224,7 @@
 
 def gradient_step(maps, measured, gate, image, wide, square, turned):
     parts, coils, planes, lines = measured.shape
-    group = math.gcd(coils, 4)
+    group = math.gcd(coils, 8)
     whole = lambda shape: pl.BlockSpec(shape, lambda i: (0,) * len(shape))
     by_coil = pl.BlockSpec((parts, group, planes, lines), lambda i: (0, i, 0, 0))
     shape = (parts, planes, lines)

time: 164 us -> 164 us (level)
  no operation moved by 1% of the time
where the time goes in v5:
time: 164 us
  Pallas kernels  142 us (87%)
  local copies, waits for them, and re-layouts  17 us (10%)
  other arithmetic  4.36 us (3%)
    pallas_call x2, Pallas kernels, exchange(): pl.pallas_call(functools.partial(exchange_kernel, size), out_shape=jax.Sh...  79.9 us
    pallas_call x2, Pallas kernels, gradient_step(): pl.pallas_call(gradient_kernel, grid=(coils // group,), in_specs=[by_coil...  29.6 us
    pallas_call x2, Pallas kernels, halos(): pl.pallas_call(functools.partial(halo_kernel, size), out_shape=jax.ShapeD...  22.1 us
    unnamed x22, local copies, waits for them, and re-layouts  14.6 us
    pallas_call x2, Pallas kernels, denoise(): pl.pallas_call(denoise_kernel, out_shape=jax.ShapeDtypeStruct(noisy.shape...  10.6 us

profile of v5, /device:TPU:0, one launch (start us, length us, event | category | flops | bytes accessed | tf_op | source)
XLA Modules:
  0.0 163.6 jit_solution(8593604680407853233)
XLA Ops:
  0.0 0.7 copy.26
  0.7 0.1 copy.28.plane_ref
  0.8 0.8 copy.27
  1.6 0.1 reshape.34.depth_ref
  1.7 1.7 %copy.29.gate_ref = s32[128,320]{1,0:T(8,128)} copy(s32[128,320]{0,1:T(8,128)} %param.13) | data formatting | bytes 327680 | tf_op args[3]
  3.4 1.0 convert_bitcast_fusion.1
  4.4 2.5 %maximum_bitcast_fusion = bf16[16,2,17,8,320]{4,0,3,2,1:T(8,128)(2,1)S(1)} fusion(bf16[2,1,8,16,320]{4,3,2,1,0:T(8,128)(2,1)S(1)} %convert_bitcast_fusion.1, bf16[2,16,8,16,320]{4,3,2,1,0:T(8,128)(2,1)} %param.11), kind=kLoop, calls=%fused_computation | loop fusion | flops 1392640 | bytes 5570560 | tf_op jit(solution)/shard_map/transpose | solution.py:348
  6.9 0.7 copy.22
  7.6 61.6 %shard_map.100 = bf16[16,272,320]{2,1,0:T(8,128)(2,1)S(1)} custom-call(bf16[16,272,320]{2,1,0:T(8,128)(2,1)S(1)} %bitcast.34), custom_call_target="tpu_custom_call" | custom-call | tf_op jit(solution)/shard_map/pallas_call | solution.py:63
  69.2 0.6 copy.36
  69.8 0.0 copy-start.8
  69.8 0.8 fusion.image_ref
  70.6 5.0 %copy.24 = bf16[2,16,128,1,320]{4,2,1,0,3:T(8,128)(2,1)} copy(bf16[2,16,128,1,320]{2,4,3,1,0:T(8,128)(2,1)} %param.10) | data formatting | bytes 5242880 | tf_op args[0]
  75.7 0.0 copy-done.8
  75.7 0.0 copy-start.7
  75.7 14.8 %shard_map.101 = (f32[2,128,320]{2,1,0:T(8,128)}, bf16[2,128,320]{2,1,0:T(8,128)(2,1)}) custom-call(bf16[2,17,128,320]{3,2,1,0:T(8,128)(2,1)} %bitcast.37, bf16[2,16,128,320]{3,2,1,0:T(8,128)(2,1)} %bitcast.39, s32[128,320]{1,0:T(8,128)} %copy.29.gate_ref, f32[2,128,320]{2,1,0:T(8,128)} %fusion.image_ref, bf16[320,704]{1,0:T(8,128)(2,1)} %constant.6.clone.wide_ref, ...), custom_call_target="tpu_custom_call" | custom-call | tf_op jit(solution)/shard_map/pallas_call | solution.py:231
  90.5 0.0 copy-start.3
  90.5 0.9 copy-done.3
  91.4 2.6 %shard_map.102.halo_ref = bf16[2,2,128,320]{3,2,1,0:T(8,128)(2,1)S(1)} custom-call(bf16[2,128,320]{2,1,0:T(8,128)(2,1)S(1)} %copy-done.3), custom_call_target="tpu_custom_call" | custom-call | tf_op jit(solution)/shard_map/pallas_call | solution.py:127
  94.0 0.0 copy-done.7
  94.0 0.0 copy-start.4
  94.0 0.9 copy-done.4
  94.9 0.0 copy-start.6
  94.9 1.0 copy-done.6
  95.9 5.3 %shard_map.103.image_ref = f32[2,128,320]{2,1,0:T(8,128)S(1)} custom-call(f32[2,128,320]{2,1,0:T(8,128)S(1)} %copy-done.6, bf16[2,128,320]{2,1,0:T(8,128)(2,1)S(1)} %copy-done.4, bf16[2,2,128,320]{3,2,1,0:T(8,128)(2,1)S(1)} %shard_map.102.halo_ref, bf16[32,18]{1,0:T(8,128)(2,1)S(1)} %copy.28.plane_ref, bf16[32,96]{1,0:T(8,128)(2,1)S(1)} %reshape.34.depth_ref, ...), custom_call_target="tpu_custom_call" | custom-call | tf_op jit(solution)/shard_map/pallas_call | solution.py:329
  101.2 0.0 copy-start
  101.2 0.8 copy-done
  102.0 14.8 %shard_map.104 = (f32[2,128,320]{2,1,0:T(8,128)}, bf16[2,128,320]{2,1,0:T(8,128)(2,1)}) custom-call(bf16[2,17,128,320]{3,2,1,0:T(8,128)(2,1)} %bitcast.38, bf16[2,16,128,320]{3,2,1,0:T(8,128)(2,1)} %bitcast.40, s32[128,320]{1,0:T(8,128)} %copy.29.gate_ref, f32[2,128,320]{2,1,0:T(8,128)} %copy-done, bf16[320,704]{1,0:T(8,128)(2,1)} %constant.6.clone.wide_ref, ...), custom_call_target="tpu_custom_call" | custom-call | tf_op jit(solution)/shard_map/pallas_call | solution.py:231
  116.8 0.0 copy-start.1
  116.8 0.9 copy-done.1
  117.7 19.5 %shard_map.105.halo_ref = bf16[2,2,128,320]{3,2,1,0:T(8,128)(2,1)S(1)} custom-call(bf16[2,128,320]{2,1,0:T(8,128)(2,1)S(1)} %copy-done.1), custom_call_target="tpu_custom_call" | custom-call | tf_op jit(solution)/shard_map/pallas_call | solution.py:127
  137.2 0.0 copy-start.2
  137.2 0.9 copy-done.2
  138.1 0.0 copy-start.5
  138.1 1.0 copy-done.5
  139.1 5.3 %shard_map.106 = f32[2,128,320]{2,1,0:T(8,128)S(1)} custom-call(f32[2,128,320]{2,1,0:T(8,128)S(1)} %copy-done.5, bf16[2,128,320]{2,1,0:T(8,128)(2,1)S(1)} %copy-done.2, bf16[2,2,128,320]{3,2,1,0:T(8,128)(2,1)S(1)} %shard_map.105.halo_ref, bf16[32,18]{1,0:T(8,128)(2,1)S(1)} %copy.28.plane_ref, bf16[32,96]{1,0:T(8,128)(2,1)S(1)} %reshape.34.depth_ref, ...), custom_call_target="tpu_custom_call" | custom-call | tf_op jit(solution)/shard_map/pallas_call | solution.py:329
  144.5 18.3 %shard_map.107 = bf16[16,16,320]{2,1,0:T(8,128)(2,1)S(1)} custom-call(bf16[16,16,320]{2,1,0:T(8,128)(2,1)S(1)} %copy_bitcast_fusion.2.sent_ref), custom_call_target="tpu_custom_call" | custom-call | tf_op jit(solution)/shard_map/pallas_call | solution.py:63
  162.8 0.9 copy.37
  (3 shorter events, 0.1 us)
Async XLA Ops:
  69.8 5.9 %copy-start.8 = (bf16[16,2,17,8,320]{4,3,0,2,1:T(8,128)(2,1)}, bf16[16,2,17,8,320]{4,3,0,2,1:T(8,128)(2,1)S(1)}, u32[]{:S(2)}) copy-start(bf16[16,2,17,8,320]{4,3,0,2,1:T(8,128)(2,1)S(1)} %copy.36) | copy-start | bytes 8355844
  75.7 18.3 %copy-start.7 = (bf16[2,32]{1,0:T(2,128)(2,1)S(1)}, bf16[2,32]{1,0:T(2,128)(2,1)}, u32[]{:S(2)}) copy-start(bf16[2,32]{1,0:T(2,128)(2,1)} %output_ref.3) | copy-start | bytes 388
  90.5 0.9 copy-start.3
  94.0 0.9 copy-start.4
  94.9 1.0 copy-start.6
  101.2 0.8 copy-start
  116.8 0.9 copy-start.1
  137.2 0.9 copy-start.2
  138.1 1.0 copy-start.5
